TPU v7x, 256 devices: a whole 4x4x8 slice. The times are simulated.
256 devices in a mesh: rep: 32 (over z, y_hi, core), tp: 8 (over x, y_lo).
Axes of the slice: x: 4, y: 4 (y_hi: 2, y_lo: 2; y = y_hi * 2 + y_lo), z: 8, core: 2. Of those that a mesh axis runs over, the one named last changes fastest.
Arguments:
- prompt: bfloat16 [32768, 8192], P('rep', 'tp'), may hold values from -6 to 6
- norm_gain: float32 [8192], replicated, may hold values from 0.1 to 1.9
- kv_weight: bfloat16 [2, 8192, 1024], P(None, None, 'tp'), may hold values from -0.0625 to 0.0625
- kv_bias: bfloat16 [2, 1024], P(None, 'tp'), may hold values from -6 to 6
- page_dest: int32 [4096, 1], P('rep'), may hold values from 0 to 31; in each aligned block of 128 rows (0 to 127, 128 to 255, ...) at most 8 rows name the same one
- page_row: int32 [4096], P('rep'), may hold values from 0 to 15
- page_offset: int32 [4096], P('rep'), may hold values from 0 to 32760
- queries: bfloat16 [512, 8192], P('rep', 'tp'), as said below
- cache_keys: bfloat16 [512, 512, 1024], P('rep', None, 'tp'), as said below
- cache_values: bfloat16 [512, 512, 1024], P('rep', None, 'tp'), may hold values from -6 to 6
- lengths: int32 [512], P('rep'), may hold values from 16 to 512, as said below
Outputs:
- attended: bfloat16 [512, 8192], P('rep', 'tp')
Inputs may be any that keep to these rules, and one draw needn't show every extreme that they name: `page_dest`: among the pages of one replica index (aligned blocks of 128 pages) no replica is named more than 8 times; some replica is named exactly 8 times. `lengths`: some row's length is exactly 512. `queries`: entries of order one to some tens. `cache_keys`: entries of order one.
All inputs are finite; a program needn't handle non-finite values.
Results may differ from a plain program's by a relative error of at most 0.018.
Values may be sent and summed in bfloat16 or wider, within the bound.
No kernel may reach another device: no remote copies, remote signals or barrier semaphores. Data moves between devices by JAX's collectives and lax.ppermute only.
A program may use at most 128 MiB of HBM per device.

v0:
```python
import jax
import jax.numpy as jnp
from jax import lax
from jax.sharding import PartitionSpec as P

Q_HEADS = 64
KV_HEADS = 8
HEAD_DIM = 128
PAGE = 8


def rotate(head_values, positions):
    half_size = head_values.shape[-1] // 2
    freq_index = jnp.arange(half_size, dtype=jnp.float32)
    inverse = jnp.exp(-(2.0 * freq_index / head_values.shape[-1]) * jnp.log(jnp.float32(1000000.0)))
    angles = positions.astype(jnp.float32)[:, None] * inverse[None, :]
    cosine = jnp.cos(angles)[:, None, :]
    sine_part = jnp.sin(angles)[:, None, :]
    first_half = head_values[..., :half_size]
    second_half = head_values[..., half_size:]
    return jnp.concatenate(
        [
            first_half * cosine - second_half * sine_part,
            second_half * cosine + first_half * sine_part,
        ],
        -1,
    )


def per_device(
    prompt,
    norm_gain,
    kv_weight,
    kv_bias,
    page_dest,
    page_row,
    page_offset,
    queries,
    cache_keys,
    cache_values,
    lengths,
):
    gathered = lax.all_gather(prompt, "tp", axis=1, tiled=True)
    values_float = gathered.astype(jnp.float32)
    inverse_rms = lax.rsqrt(jnp.mean(values_float * values_float, -1, keepdims=True) + 1e-06)
    normed = (values_float * inverse_rms * norm_gain).astype(jnp.bfloat16)
    projected = jnp.einsum("td,sdc->stc", normed, kv_weight, preferred_element_type=jnp.float32)
    projected = projected + kv_bias.astype(jnp.float32)[:, None, :]
    token_count = projected.shape[1]
    page_count = page_offset.shape[0]
    local_heads = projected.shape[2] // HEAD_DIM
    positions = jnp.repeat(page_offset, PAGE) + jnp.tile(
        jnp.arange(PAGE, dtype=jnp.int32), page_count
    )
    key_heads = projected[0].reshape(token_count, local_heads, HEAD_DIM)
    new_keys = rotate(key_heads, positions).reshape(token_count, -1).astype(jnp.bfloat16)
    new_values = projected[1].astype(jnp.bfloat16)
    key_width = new_keys.shape[1]
    packed = jnp.concatenate([new_keys, new_values], 1)
    row_count = queries.shape[0]
    groups = Q_HEADS // KV_HEADS
    score_scale = HEAD_DIM ** (-0.5)
    row_ids = jnp.arange(row_count, dtype=jnp.int32)
    query_heads = queries.reshape(row_count, local_heads, groups, HEAD_DIM)
    cache_k = cache_keys.reshape(row_count, -1, local_heads, HEAD_DIM)
    cache_v = cache_values.reshape(row_count, -1, local_heads, HEAD_DIM)
    resident = (
        jnp.einsum("bhgd,bthd->bhgt", query_heads, cache_k, preferred_element_type=jnp.float32)
        * score_scale
    )
    live_mask = jnp.arange(cache_k.shape[1], dtype=jnp.int32)[None, :] < lengths[:, None]
    resident = jnp.where(live_mask[:, None, None, :], resident, -1e30)
    resident_top = jnp.max(resident, -1)
    own_index = lax.axis_index("rep")
    token_meta = jnp.stack([jnp.repeat(page_dest[:, 0], PAGE), jnp.repeat(page_row, PAGE)], 1)
    weight_res = jnp.exp(resident - resident_top[..., None])
    total_start = jnp.sum(weight_res, -1)
    summed_start = jnp.einsum(
        "bhgt,bthd->bhgd",
        weight_res.astype(jnp.bfloat16),
        cache_v,
        preferred_element_type=jnp.float32,
    )
    piece_data = lax.all_gather(packed, "rep", axis=0, tiled=True)
    piece_meta = lax.all_gather(token_meta, "rep", axis=0, tiled=True)
    keys_piece = piece_data[:, :key_width].reshape(-1, local_heads, HEAD_DIM)
    values_piece = piece_data[:, key_width:].reshape(-1, local_heads, HEAD_DIM)
    owned_mask = (piece_meta[:, 0][None, :] == own_index) & (
        piece_meta[:, 1][None, :] == row_ids[:, None]
    )
    piece_scores = (
        jnp.einsum("bhgd,nhd->bhgn", query_heads, keys_piece, preferred_element_type=jnp.float32)
        * score_scale
    )
    piece_scores = jnp.where(owned_mask[:, None, None, :], piece_scores, -1e30)
    top_new = jnp.maximum(resident_top, jnp.max(piece_scores, -1))
    shrink = jnp.exp(resident_top - top_new)
    piece_weights = jnp.exp(piece_scores - top_new[..., None])
    total_new = total_start * shrink + jnp.sum(piece_weights, -1)
    summed_new = summed_start * shrink[..., None] + jnp.einsum(
        "bhgn,nhd->bhgd",
        piece_weights.astype(jnp.bfloat16),
        values_piece,
        preferred_element_type=jnp.float32,
    )
    return (summed_new / total_new[..., None]).reshape(row_count, -1).astype(jnp.bfloat16)


def solution(mesh):
    placed = (
        P("rep", "tp"),
        P(),
        P(None, None, "tp"),
        P(None, "tp"),
        P("rep", None),
        P("rep"),
        P("rep"),
        P("rep", "tp"),
        P("rep", None, "tp"),
        P("rep", None, "tp"),
        P("rep"),
    )
    return jax.shard_map(
        per_device, mesh=mesh, in_specs=placed, out_specs=P("rep", "tp"), check_vma=False
    )
```

profile of v0, /device:TPU:8, one launch (start us, length us, event | category | flops | bytes accessed | tf_op | source)
XLA Modules:
  0.0 528.9 jit_solution(17899314666299356936)
XLA Ops:
  6.5 0.0 copy-start
  6.5 0.0 all-gather.3.cloned.1.call-start
  6.5 0.7 all-gather.3.cloned.1.call-update
  7.3 0.0 all-gather.5.cloned.1.call-start
  7.3 6.4 %copy.40 = bf16[2,8192,128]{1,2,0:T(8,128)(2,1)} copy(bf16[2,8192,128]{2,1,0:T(8,128)(2,1)} %param.13) | data formatting | bytes 8388608 | tf_op args[2]
  13.7 0.7 convert_element_type.43
  14.3 0.7 add_convert_fusion
  15.1 0.1 convert_element_type.45
  15.2 324.0 %all-gather.3.cloned.1.call-done = bf16[1024,8192]{1,0:T(8,128)(2,1)} async-done(((bf16[1024,1024]{1,0:T(8,128)(2,1)}), bf16[1024,8192]{1,0:T(8,128)(2,1)}) %all-gather.3.cloned.1.call-update) | async-done | bytes 16777232 | tf_op jit(solution)/shard_map/all_gather | solution.py:43
  339.1 7.5 %fusion.2 = f32[1024]{0:T(1024)S(1)} fusion(bf16[1024,8192]{1,0:T(8,128)(2,1)} %all-gather.3.cloned.1.call-done), kind=kLoop, calls=%fused_computation.5 | loop fusion | flops 25164800 | bytes 16781312 | tf_op jit(solution)/shard_map/reduce_sum | solution.py:45
  346.6 0.0 copy-done.8
  346.6 0.0 copy-done.2
  346.7 0.0 copy-start.5
  346.7 0.0 copy-start.6
  346.7 0.0 copy-start.4
  346.7 0.0 copy-start.7
  346.7 8.6 %fusion.5 = f32[1024,256]{0,1:S(1)} fusion(bf16[8192,256]{0,1:T(8,128)(2,1)S(1)} %bitcast.65, bf16[1024,8192]{1,0:T(8,128)(2,1)} %all-gather.3.cloned.1.call-done, f32[8192]{0:T(1024)S(1)} %copy-done.8, f32[1024]{0:T(1024)S(1)} %add_rsqrt_fusion), kind=kOutput, calls=%fused_computation.8 | convolution fusion | flops 4328521728 | bytes 22056960
  355.3 0.1 add_bitcast_fusion
  355.5 1.2 fusion.28
  356.7 0.8 pad_maximum_fusion
  357.6 0.0 all-gather.5.cloned.1.call-update
  357.6 0.0 copy-done.5
  357.6 0.1 broadcast_in_dim.32
  357.7 0.1 stack_reshape.6
  357.8 0.0 copy-done.6
  357.8 0.1 broadcast_in_dim.33
  357.9 0.1 stack_reshape.7
  358.0 42.8 %all_gather.9 = s32[32768,2]{0,1:T(2,128)S(1)} all-gather(s32[1024,2]{0,1:T(2,128)S(1)} %pad_add_fusion), channel_id=1, replica_groups=mesh['rep'=32,'tp'=8] {'rep'}, dimensions={0}, use_global_device_ids=true | all-gather | bytes 270336 | tf_op jit(solution)/shard_map/all_gather | solution.py:85
  400.8 0.1 slice.34
  400.9 0.0 copy-done.4
  400.9 0.0 copy-done.7
  400.9 0.1 iota_compare_fusion.1
  401.0 0.0 copy-done
  401.0 0.7 fusion.38
  401.8 0.1 copy.44
  401.8 0.2 fusion.32
  402.0 0.1 copy.48
  402.1 0.4 compare_reduce_fusion
  402.5 0.4 fusion.14
  402.9 94.2 %all-gather.5.cloned.1.call-done = bf16[32768,256]{0,1:T(8,128)(2,1)} async-done(((bf16[1024,256]{0,1:T(8,128)(2,1)}), bf16[32768,256]{0,1:T(8,128)(2,1)}) %all-gather.5.cloned.1.call-update) | async-done | bytes 16777232 | tf_op jit(solution)/shard_map/all_gather | solution.py:84
  497.1 5.8 %fusion.39 = (f32[16,8]{0,1:T(8,128)S(1)}, f32[16,1,8,32768]{3,0,2,1:T(8,128)S(1)}) fusion(bf16[32768,256]{0,1:T(8,128)(2,1)} %all-gather.5.cloned.1.call-done, pred[16,32768]{1,0:T(8,128)(4,1)S(1)} %fusion.14, bf16[16,1024]{1,0:T(8,128)(2,1)S(1)} %copy-done.4), kind=kOutput, calls=%fused_computation.61 | convolution fusion | flops 1086324608 | bytes 25723392 | tf_op jit(solution)/shard_map/bhgd,nhd->bhgn/dot_general | solution.py:92
  502.9 6.5 %fusion.9 = (f32[16,8]{0,1:T(8,128)S(1)}, bf16[16,8,32768]{2,0,1:T(8,128)(2,1)}) fusion(f32[16,1,8,32768]{3,0,2,1:T(8,128)S(1)} %get-tuple-element.14, f32[16,8]{0,1:T(8,128)S(1)} %max.17), kind=kLoop, calls=%fused_computation.12 | loop fusion | flops 12582784 | bytes 25166848 | tf_op jit(solution)/shard_map/reduce_sum | solution.py:99
  509.4 0.1 copy.45
  509.5 0.1 copy.49
  509.6 11.4 %fusion.16 = f32[16,1,8,128]{3,2,0,1:T(8,128)S(1)} fusion(bf16[16,8,32768]{2,0,1:T(8,128)(2,1)} %get-tuple-element.8, bf16[32768,256]{0,1:T(8,128)(2,1)} %all-gather.5.cloned.1.call-done), kind=kOutput, calls=%fused_computation.23 | convolution fusion | flops 1073741824 | bytes 16842752 | tf_op jit(solution)/shard_map/bhgn,nhd->bhgd/dot_general | solution.py:100
  521.0 0.0 copy-done.3
  521.0 0.4 fusion.22
  521.5 0.6 copy.70
  (14 shorter events, 0.1 us)
Async XLA Ops:
  6.5 394.5 %copy-start = (bf16[16,512,128]{2,1,0:T(8,128)(2,1)S(1)}, bf16[16,512,128]{2,1,0:T(8,128)(2,1)}, u32[]{:S(2)}) copy-start(bf16[16,512,128]{2,1,0:T(8,128)(2,1)} %param.19) | copy-start | bytes 6291460
  6.5 340.1 %copy-start.8 = (f32[8192]{0:T(1024)S(1)}, f32[8192]{0:T(1024)}, u32[]{:S(2)}) copy-start(f32[8192]{0:T(1024)} %param.12) | copy-start | bytes 98308
  6.5 332.6 %all-gather.3.cloned.1.call-start = ((), (), s32[]{:S(2)}) async-start(), calls=%async_computation | async-start | bytes 18874368 | tf_op jit(solution)/shard_map/all_gather | solution.py:43
  7.3 489.9 %all-gather.5.cloned.1.call-start = ((), (), s32[]{:S(2)}) async-start(), calls=%async_computation.1 | async-start | bytes 17301504 | tf_op jit(solution)/shard_map/all_gather | solution.py:84
  339.1 7.5 %copy-start.2 = (bf16[2,8192,128]{1,2,0:T(8,128)(2,1)S(1)}, bf16[2,8192,128]{1,2,0:T(8,128)(2,1)}, u32[]{:S(2)}) copy-start(bf16[2,8192,128]{1,2,0:T(8,128)(2,1)} %copy.40) | copy-start | bytes 12582916
  346.7 10.9 %copy-start.5 = (s32[128,1]{0,1:T(1,128)S(1)}, s32[128,1]{0,1:T(1,128)}, u32[]{:S(2)}) copy-start(s32[128,1]{0,1:T(1,128)} %param.15) | copy-start | bytes 1540
  346.7 11.1 %copy-start.6 = (s32[128]{0:T(128)S(1)}, s32[128]{0:T(128)}, u32[]{:S(2)}) copy-start(s32[128]{0:T(128)} %param.16) | copy-start | bytes 1540
  346.7 54.2 %copy-start.4 = (bf16[16,1024]{1,0:T(8,128)(2,1)S(1)}, bf16[16,1024]{1,0:T(8,128)(2,1)}, u32[]{:S(2)}) copy-start(bf16[16,1024]{1,0:T(8,128)(2,1)} %param.18) | copy-start | bytes 98308
  346.7 54.2 %copy-start.7 = (s32[16]{0:T(128)S(1)}, s32[16]{0:T(128)}, u32[]{:S(2)}) copy-start(s32[16]{0:T(128)} %param.21) | copy-start | bytes 196
  509.6 11.4 %copy-start.3 = (bf16[16,512,128]{2,1,0:T(8,128)(2,1)S(1)}, bf16[16,512,128]{2,1,0:T(8,128)(2,1)}, u32[]{:S(2)}) copy-start(bf16[16,512,128]{2,1,0:T(8,128)(2,1)} %param.20) | copy-start | bytes 6291460
  509.6 12.5 %copy-start.1 = (bf16[16,512,128]{2,1,0:T(8,128)(2,1)S(1)}, bf16[16,512,128]{2,1,0:T(8,128)(2,1)}, u32[]{:S(2)}) copy-start(bf16[16,512,128]{2,1,0:T(8,128)(2,1)} %param.19) | copy-start | bytes 6291460
Sparse Core Ops, SparseCore 0:
  9.2 329.9 all-gather.2
  357.7 139.3 all-gather.4
where the time goes:
time: 531 us; the launch traced here: 529 us
  waiting for transfers between devices  419 us (79%)
  blocking collectives  42.8 us (8%)
  matrix products  27 us (5%)
  other arithmetic  18.6 us (4%)
  between operations  13.7 us (3%)
  local copies, waits for them, and re-layouts  8 us (2%)
    all_gather x1, waiting for transfers between devices, per_device(): gathered = lax.all_gather(prompt, 'tp', axis=1, tiled=True)  324 us
    all_gather x1, waiting for transfers between devices, per_device(): piece_data = lax.all_gather(packed, 'rep', axis=0, tiled=True)  94.2 us
    all_gather x1, blocking collectives, per_device(): piece_meta = lax.all_gather(token_meta, 'rep', axis=0, tiled=True)  42.8 us
    dot_general x1, matrix products, per_device(): jnp.einsum('bhgn,nhd->bhgd', piece_weights.astype(jnp.bfloat16), values_p...  11.4 us
  transfers between devices with their start and end apart: 2, of which 2 were waited for; matrix products, arithmetic and copies ran while one was open for 2% of the time, Pallas kernels for 0%

commit v1 on v0

v1 whole, which is shorter than its diff:
```python
import functools

import jax
import jax.numpy as jnp
from jax import lax
from jax.experimental import pallas as pl
from jax.experimental.pallas import tpu as pltpu
from jax.sharding import PartitionSpec as P

D = 8192
HEAD_DIM = 128
PAGE = 8
TOK = 1024
FEAT = 1024
REPLICAS = 32
SLOTS = 8
ROWS = 16
GROUPS = 8
CONTEXT = 512
TILE = 256
STAT = 16
LOW = -1e30
MIB = 1 << 20
NT = (((1,), (1,)), ((), ()))
TN = (((0,), (0,)), ((), ()))
F32 = jnp.float32
BF16 = jnp.bfloat16
VMEM = pl.BlockSpec(memory_space=pltpu.VMEM)
SMEM = pl.BlockSpec(memory_space=pltpu.SMEM)


def cost(flops, bytes_accessed):
    return pl.CostEstimate(flops=flops, bytes_accessed=bytes_accessed, transcendentals=0)


def params(mib):
    return pltpu.CompilerParams(vmem_limit_bytes=mib * MIB)


def device_number(x, y_lo, z, y_hi, core):
    return ((z * 2 + y_hi) * 2 + core) * 8 + x * 2 + y_lo


def permute(array, target):
    pairs = [
        (device_number(x, y, z, h, c), device_number(*target(x, y, z, h, c)))
        for x in range(4)
        for y in range(2)
        for z in range(8)
        for h in range(2)
        for c in range(2)
    ]
    return lax.ppermute(array, ("rep", "tp"), pairs)


def prepare_kernel(own_slot, own, other, gain, first, second, squares_first, squares_second):
    tile = pl.program_id(0)
    ones = jnp.ones((8, FEAT), BF16)

    def scaled(ref):
        values = ref[...].astype(F32)
        return (values * gain[...]).astype(BF16)

    def squares(ref):
        values = ref[...].astype(F32)
        square = values * values
        high = square.astype(BF16)
        low = (square - high.astype(F32)).astype(BF16)
        total = lax.dot_general(ones, high, NT, preferred_element_type=F32)
        total = total + lax.dot_general(ones, low, NT, preferred_element_type=F32)
        total = total[0:1, :]
        top = total.astype(BF16).astype(F32)
        rest = (total - top).astype(BF16).astype(F32)
        return top, rest

    def write(source_a, source_b):
        first[...] = scaled(source_a)
        second[...] = scaled(source_b)
        for source, out in ((source_a, squares_first), (source_b, squares_second)):
            top, rest = squares(source)
            out[pl.ds(tile, 1), :] = top
            out[pl.ds(tile + 4, 1), :] = rest

    @pl.when(tile == 0)
    def _():
        squares_first[...] = jnp.zeros_like(squares_first)
        squares_second[...] = jnp.zeros_like(squares_second)

    @pl.when(own_slot[0] == 0)
    def _():
        write(own, other)

    @pl.when(own_slot[0] != 0)
    def _():
        write(other, own)


def prepare(own_slot, own, other, gain):
    tokens = pl.BlockSpec((TILE, FEAT), lambda i: (i, 0))
    squares = pl.BlockSpec((STAT, TILE), lambda i: (0, 0))
    return pl.pallas_call(
        prepare_kernel,
        grid=(TOK // TILE,),
        in_specs=[SMEM, tokens, tokens, pl.BlockSpec((1, FEAT), lambda i: (0, 0))],
        out_specs=[tokens, tokens, squares, squares],
        out_shape=[
            jax.ShapeDtypeStruct((TOK, FEAT), BF16),
            jax.ShapeDtypeStruct((TOK, FEAT), BF16),
            jax.ShapeDtypeStruct((STAT, TILE), F32),
            jax.ShapeDtypeStruct((STAT, TILE), F32),
        ],
        compiler_params=params(24),
        cost_estimate=cost(16 * TOK * FEAT, 8 * MIB),
        name="prepare",
    )(own_slot, own, other, gain)


def project_kernel(tokens, squares, weight, out):
    tile = pl.program_id(0)
    both = jnp.concatenate([weight[0], weight[1]], axis=1)
    part = lax.dot_general(tokens[...], both, (((1,), (0,)), ((), ())), preferred_element_type=F32)
    out[pl.ds(pl.multiple_of(tile * TILE, TILE), TILE), :] = part.astype(BF16)

    @pl.when(tile == 0)
    def _():
        out[TOK : TOK + STAT, :] = squares[...].astype(BF16)


def project(tokens, squares, weight):
    return pl.pallas_call(
        project_kernel,
        grid=(TOK // TILE,),
        in_specs=[
            pl.BlockSpec((TILE, FEAT), lambda i: (i, 0)),
            pl.BlockSpec((STAT, TILE), lambda i: (0, 0)),
            pl.BlockSpec((2, FEAT, HEAD_DIM), lambda i: (0, 0, 0)),
        ],
        out_specs=pl.BlockSpec((TOK + STAT, 2 * HEAD_DIM), lambda i: (0, 0)),
        out_shape=jax.ShapeDtypeStruct((TOK + STAT, 2 * HEAD_DIM), BF16),
        compiler_params=params(16),
        cost_estimate=cost(2 * TOK * FEAT * 2 * HEAD_DIM, 3 * MIB),
        name="project",
    )(tokens, squares, weight)


def resident_kernel(lengths, queries, keys, values, out, top_out, total_out, sums, tops, totals):
    row = pl.program_id(0)
    scores = lax.dot_general(queries[...], keys[0], NT, preferred_element_type=F32)
    scores = scores * HEAD_DIM**-0.5
    slot = lax.broadcasted_iota(jnp.int32, scores.shape, 1)
    scores = jnp.where(slot < lengths[row], scores, LOW)
    top = jnp.max(scores, axis=1, keepdims=True)
    weights = jnp.exp(scores - top)
    total = jnp.sum(weights, axis=1, keepdims=True)
    place = pl.ds(pl.multiple_of(row * GROUPS, GROUPS), GROUPS)
    sums[place, :] = jnp.dot(weights.astype(BF16), values[0], preferred_element_type=F32)
    tops[place, :] = jnp.broadcast_to(top, (GROUPS, HEAD_DIM))
    totals[place, :] = jnp.broadcast_to(total, (GROUPS, HEAD_DIM))

    @pl.when(row == ROWS - 1)
    def _():
        out[...] = sums[...].T
        top_out[...] = tops[...].T[0:8]
        total_out[...] = totals[...].T[0:8]


def resident(lengths, queries, keys, values):
    cache = pl.BlockSpec((1, CONTEXT, HEAD_DIM), lambda i: (i, 0, 0))
    whole = pl.BlockSpec((HEAD_DIM, HEAD_DIM), lambda i: (0, 0))
    stat = pl.BlockSpec((8, HEAD_DIM), lambda i: (0, 0))
    return pl.pallas_call(
        resident_kernel,
        grid=(ROWS,),
        in_specs=[SMEM, pl.BlockSpec((GROUPS, HEAD_DIM), lambda i: (i, 0)), cache, cache],
        out_specs=[whole, stat, stat],
        out_shape=[
            jax.ShapeDtypeStruct((HEAD_DIM, HEAD_DIM), F32),
            jax.ShapeDtypeStruct((8, HEAD_DIM), F32),
            jax.ShapeDtypeStruct((8, HEAD_DIM), F32),
        ],
        scratch_shapes=[pltpu.VMEM((HEAD_DIM, HEAD_DIM), F32)] * 3,
        compiler_params=params(16),
        cost_estimate=cost(4 * ROWS * GROUPS * CONTEXT * HEAD_DIM, 16 * MIB),
        name="resident",
    )(lengths, queries, keys, values)


def split_stats(top, total):
    top_a = top.astype(BF16).astype(F32)
    top_b = (top - top_a).astype(BF16).astype(F32)
    top_c = (top - top_a) - top_b
    total_a = total.astype(BF16).astype(F32)
    total_b = total - total_a
    rows = [top_a, top_b, top_c, total_a, total_b]
    index = lax.broadcasted_iota(jnp.int32, (STAT, HEAD_DIM), 0)
    tile = jnp.zeros((STAT, HEAD_DIM), F32)
    for number, row in enumerate(rows):
        tile = jnp.where(index == number, row, tile)
    return tile.astype(BF16)


def join_stats(tile):
    stats = tile.astype(F32)
    top = (stats[0:1] + stats[1:2]) + stats[2:3]
    return top, stats[3:4] + stats[4:5]


def finish_kernel(pages, page_rows, core, *refs):
    parts = refs[:8]
    cosine, sine, bias, queries, kept, sent, key_store, value_store = refs[8:]
    squares = jnp.concatenate([part[TOK : TOK + STAT, :] for part in parts], axis=0)
    index = lax.broadcasted_iota(jnp.int32, (8 * STAT, HEAD_DIM), 0)
    for tile in range(TOK // TILE):
        token = slice(tile * TILE, (tile + 1) * TILE)
        chosen = ((index % STAT) < 8) & ((index % 4) == tile)
        total = lax.dot_general(
            squares, jnp.where(chosen, 1.0, 0.0).astype(BF16), TN, preferred_element_type=F32
        )
        inverse = lax.rsqrt(total * (1.0 / D) + 1e-06)
        added = parts[0][token, :].astype(F32)
        for part in parts[1:]:
            added = added + part[token, :].astype(F32)
        keys = added[:, :HEAD_DIM] * inverse + bias[0:1, :]
        values = added[:, HEAD_DIM:] * inverse + bias[1:2, :]
        keys = keys * cosine[token, :] + pltpu.roll(keys, HEAD_DIM // 2, 1) * sine[token, :]
        key_store[token, :] = keys.astype(BF16).astype(F32)
        value_store[token, :] = values.astype(BF16).astype(F32)

    lane_row = lax.broadcasted_iota(jnp.int32, (PAGE, HEAD_DIM), 1) // GROUPS

    def attend(replica):
        key_pages, value_pages, masks = [], [], []
        for slot in range(SLOTS):
            page = pages[replica * SLOTS + slot]
            place = pl.ds(pl.multiple_of(page * PAGE, PAGE), PAGE)
            key_pages.append(key_store[place, :])
            value_pages.append(value_store[place, :])
            masks.append(lane_row == page_rows[replica * SLOTS + slot])
        keys = jnp.concatenate(key_pages, axis=0).astype(BF16)
        values = jnp.concatenate(value_pages, axis=0).astype(BF16)
        scores = lax.dot_general(keys, queries[replica], NT, preferred_element_type=F32)
        scores = scores * HEAD_DIM**-0.5
        scores = jnp.where(jnp.concatenate(masks, axis=0), scores, LOW)
        top = jnp.max(scores, axis=0, keepdims=True)
        weights = jnp.exp(scores - top)
        total = jnp.sum(weights, axis=0, keepdims=True)
        summed = lax.dot_general(values, weights.astype(BF16), TN, preferred_element_type=F32)
        return summed.astype(BF16), split_stats(top, total)

    for flip, out in ((1, sent), (0, kept)):

        def block(step, carry, flip=flip, out=out):
            for inner in range(4):
                place = step * 4 + inner
                replica = place * 2 + (core[0] + flip) % 2
                summed, stats = attend(replica)
                out[place, 0:HEAD_DIM, :] = summed
                out[place, HEAD_DIM : HEAD_DIM + STAT, :] = stats
            return carry

        lax.fori_loop(0, 4, block, 0)


def finish(pages, page_rows, core, parts, cosine, sine, bias, queries):
    partial = jax.ShapeDtypeStruct((16, HEAD_DIM + STAT, HEAD_DIM), BF16)
    return pl.pallas_call(
        finish_kernel,
        in_specs=[SMEM] * 3 + [VMEM] * 12,
        out_specs=[VMEM, VMEM],
        out_shape=[partial, partial],
        scratch_shapes=[pltpu.VMEM((TOK, HEAD_DIM), F32)] * 2,
        compiler_params=params(32),
        cost_estimate=cost(4 * 2048 * 128 * 128, 16 * MIB),
        name="finish",
    )(pages, page_rows, core, *parts, cosine, sine, bias, queries)


def merge_kernel(left, right, out):
    def block(step, carry):
        for inner in range(4):
            place = step * 4 + inner
            left_top, left_total = join_stats(left[place, HEAD_DIM:, :])
            right_top, right_total = join_stats(right[place, HEAD_DIM:, :])
            top = jnp.maximum(left_top, right_top)
            left_scale = jnp.exp(left_top - top)
            right_scale = jnp.exp(right_top - top)
            summed = left[place, 0:HEAD_DIM, :].astype(F32) * left_scale
            summed = summed + right[place, 0:HEAD_DIM, :].astype(F32) * right_scale
            out[place, 0:HEAD_DIM, :] = summed.astype(BF16)
            total = left_total * left_scale + right_total * right_scale
            out[place, HEAD_DIM:, :] = split_stats(top, total)
        return carry

    lax.fori_loop(0, 4, block, 0)


def merge(left, right):
    return pl.pallas_call(
        merge_kernel,
        in_specs=[VMEM, VMEM],
        out_specs=VMEM,
        out_shape=jax.ShapeDtypeStruct((16, HEAD_DIM + STAT, HEAD_DIM), BF16),
        compiler_params=params(16),
        cost_estimate=cost(16 * 128 * 128 * 4, 2 * MIB),
        name="merge",
    )(left, right)


def conclude_kernel(received, sums, tops, totals, out, store):
    stats = [join_stats(received[i, HEAD_DIM:, :]) for i in range(16)]
    top = tops[0:1]
    for part_top, _ in stats:
        top = jnp.maximum(top, part_top)
    scale = jnp.exp(tops[0:1] - top)
    summed = sums[...] * scale
    total = totals[0:1] * scale
    for i, (part_top, part_total) in enumerate(stats):
        scale = jnp.exp(part_top - top)
        summed = summed + received[i, 0:HEAD_DIM, :].astype(F32) * scale
        total = total + part_total * scale
    store[...] = (summed / total).T
    for group in range(GROUPS):
        columns = slice(group * HEAD_DIM, (group + 1) * HEAD_DIM)
        out[:, columns] = store[pl.ds(group, ROWS, stride=GROUPS), :].astype(BF16)


def conclude(received, sums, tops, totals):
    return pl.pallas_call(
        conclude_kernel,
        in_specs=[VMEM] * 4,
        out_specs=VMEM,
        out_shape=jax.ShapeDtypeStruct((ROWS, GROUPS * HEAD_DIM), BF16),
        scratch_shapes=[pltpu.VMEM((HEAD_DIM, HEAD_DIM), F32)],
        compiler_params=params(16),
        cost_estimate=cost(16 * 128 * 128 * 4, MIB),
        name="conclude",
    )(received, sums, tops, totals)


def angle_tables(page_offset):
    half = HEAD_DIM // 2
    index = jnp.arange(half, dtype=F32)
    inverse = jnp.exp(-(2.0 * index / HEAD_DIM) * jnp.log(F32(1000000.0)))
    positions = jnp.repeat(page_offset, PAGE) + jnp.tile(
        jnp.arange(PAGE, dtype=jnp.int32), page_offset.shape[0]
    )
    angles = positions.astype(F32)[:, None] * inverse[None, :]
    cosine, sine = jnp.cos(angles), jnp.sin(angles)
    return jnp.concatenate([cosine, cosine], 1), jnp.concatenate([-sine, sine], 1)


def page_tables(page_dest, page_row):
    dest = page_dest[:, 0]
    count = dest.shape[0]
    number = jnp.arange(count, dtype=jnp.int32)
    earlier = (dest[None, :] == dest[:, None]) & (number[None, :] < number[:, None])
    slot = dest * SLOTS + jnp.sum(earlier.astype(jnp.int32), 1)
    match = slot[None, :] == jnp.arange(REPLICAS * SLOTS, dtype=jnp.int32)[:, None]
    pages = jnp.max(jnp.where(match, number[None, :], 0), 1)
    rows = jnp.max(jnp.where(match, page_row[None, :], -1), 1)
    return pages, rows


def per_device(
    prompt,
    norm_gain,
    kv_weight,
    kv_bias,
    page_dest,
    page_row,
    page_offset,
    queries,
    cache_keys,
    cache_values,
    lengths,
):
    tp = lax.axis_index("tp")
    core = lax.axis_index("rep") % 2
    x, y = tp // 2, tp % 2
    query_heads = queries.reshape(ROWS * GROUPS, HEAD_DIM)
    all_queries = lax.all_gather(query_heads, "rep", axis=0, tiled=False)
    other = permute(prompt, lambda x, y, z, h, c: (x, y, z, h, 1 - c))

    order = (2, 1, 3, 0)
    weights = {}
    for dx in order:
        block = ((x + dx) % 4) * 2 + (y + core) % 2
        rows = lax.dynamic_slice(kv_weight, (0, block * FEAT, 0), (2, FEAT, HEAD_DIM))
        weights[dx] = permute(rows, lambda x, y, z, h, c, dx=dx: ((x + dx) % 4, y ^ c, z, h, y))

    gain = lax.dynamic_slice(norm_gain, (tp * FEAT,), (FEAT,)).reshape(1, FEAT)
    own_slot = ((y + core) % 2).reshape(1)
    first, second, squares_first, squares_second = prepare(own_slot, prompt, other, gain)
    tokens, squares = (first, second), (squares_first, squares_second)

    sums, tops, totals = resident(lengths, query_heads, cache_keys, cache_values)
    cosine, sine = angle_tables(page_offset)
    pages, page_rows = page_tables(page_dest, page_row)

    parts = []
    for dx in order:
        for k in range(2):
            part = project(tokens[k], squares[k], weights[dx])
            parts.append(
                permute(part, lambda x, y, z, h, c, dx=dx, k=k: ((x - dx) % 4, c, z, h, y ^ k))
            )

    kept, sent = finish(
        pages, page_rows, core.reshape(1), parts, cosine, sine, kv_bias.astype(F32), all_queries
    )
    arrived = permute(sent, lambda x, y, z, h, c: (x, y, z, h, 1 - c))
    merged = merge(kept, arrived)
    groups = [[zy * 2 + c for zy in range(16)] for c in range(2)]
    received = lax.all_to_all(merged, "rep", 0, 0, tiled=True, axis_index_groups=groups)
    return conclude(received, sums, tops, totals)


def solution(mesh):
    placed = (
        P("rep", "tp"),
        P(),
        P(None, None, "tp"),
        P(None, "tp"),
        P("rep", None),
        P("rep"),
        P("rep"),
        P("rep", "tp"),
        P("rep", None, "tp"),
        P("rep", None, "tp"),
        P("rep"),
    )
    return jax.shard_map(
        per_device, mesh=mesh, in_specs=placed, out_specs=P("rep", "tp"), check_vma=False
    )
```

time: 531 us -> 168 us (0.32)
  waiting for transfers between devices: 419 us -> 71.2 us
  blocking collectives: 42.8 us -> 0 us
  Pallas kernels: 0 us -> 40.1 us
  matrix products: 27 us -> 0 us
  starting transfers between devices: 0.04 us -> 26.7 us
  other arithmetic: 18.6 us -> 2.66 us
    all_gather x2 -> x1, waiting for transfers between devices: 418 us -> 45.6 us  [per_device(): all_queries = lax.all_gather(query_heads, 'rep', axis=0, tiled=False)]
    all_gather x1 -> x0, blocking collectives: 42.8 us -> none  [per_device(): piece_meta = lax.all_gather(token_meta, 'rep', axis=0, tiled=True)]
    pallas_call x0 -> x13, Pallas kernels: none -> 40.1 us  [the longest x8 16.7 us: project(): pl.pallas_call(project_kernel, grid=(TOK // TILE,), in_specs=[pl.BlockSpe...]
    ppermute x0 -> x14, starting transfers between devices: none -> 22.3 us  [permute(): return lax.ppermute(array, ('rep', 'tp'), pairs)]
    dot_general x4 -> x0, matrix products: 18.4 us -> none  [the longest x1 11.4 us: per_device(): jnp.einsum('bhgn,nhd->bhgd', piece_weights.astype(jnp.bfloat16), values_p...]
    reduce_sum x3 -> x1, other arithmetic: 14.1 us -> 0.17 us  [page_tables(): slot = dest * SLOTS + jnp.sum(earlier.astype(jnp.int32), 1)]
    all_to_all x0 -> x1, waiting for transfers between devices: none -> 12.8 us  [per_device(): lax.all_to_all(merged, 'rep', 0, 0, tiled=True, axis_index_groups=groups)]
    ppermute x0 -> x14, waiting for transfers between devices: none -> 12.7 us  [permute(): return lax.ppermute(array, ('rep', 'tp'), pairs)]
  transfers between devices with their start and end apart: 2 -> 16, of which waited for: 2 -> 4; matrix products, arithmetic and copies ran while one was open for 2% -> 5% of each run, Pallas kernels for 0% -> 17%
where the time goes in v1:
time: 168 us; the launch traced here: 167 us
  waiting for transfers between devices  71.2 us (42%)
  Pallas kernels  40.1 us (24%)
  starting transfers between devices  26.7 us (16%)
  between operations  13.9 us (8%)
  local copies, waits for them, and re-layouts  12.6 us (8%)
  other arithmetic  2.66 us (2%)
    all_gather x1, waiting for transfers between devices, per_device(): all_queries = lax.all_gather(query_heads, 'rep', axis=0, tiled=False)  45.6 us
    ppermute x14, starting transfers between devices, permute(): return lax.ppermute(array, ('rep', 'tp'), pairs)  22.3 us
    pallas_call x8, Pallas kernels, project(): pl.pallas_call(project_kernel, grid=(TOK // TILE,), in_specs=[pl.BlockSpe...  16.7 us
    all_to_all x1, waiting for transfers between devices, per_device(): lax.all_to_all(merged, 'rep', 0, 0, tiled=True, axis_index_groups=groups)  12.8 us
    ppermute x14, waiting for transfers between devices, permute(): return lax.ppermute(array, ('rep', 'tp'), pairs)  12.7 us
    pallas_call x1, Pallas kernels, finish(): pl.pallas_call(finish_kernel, in_specs=[SMEM] * 3 + [VMEM] * 12, out_spec...  9.57 us
    unnamed x32, local copies, waits for them, and re-layouts  7.33 us
    pallas_call x1, Pallas kernels, resident(): pl.pallas_call(resident_kernel, grid=(ROWS,), in_specs=[SMEM, pl.BlockSpe...  6.48 us
  transfers between devices with their start and end apart: 16, of which 4 were waited for; matrix products, arithmetic and copies ran while one was open for 5% of the time, Pallas kernels for 17%

profile of v1, /device:TPU:8, one launch (start us, length us, event | category | flops | bytes accessed | tf_op | source)
XLA Modules:
  0.0 167.1 jit_solution(11464295114144071945)
XLA Ops:
  6.5 1.4 all_gather_reshape.3
  7.9 0.0 all-gather.2.cloned.1.call-update
  8.1 0.0 copy-start.14
  8.1 3.1 %constant_dynamic-slice_fusion = (bf16[2,1024,128]{2,1,0:T(8,128)(2,1)}, bf16[2,1024,128]{2,1,0:T(8,128)(2,1)}, bf16[2,1024,128]{2,1,0:T(8,128)(2,1)}, bf16[2,1024,128]{2,1,0:T(8,128)(2,1)}) fusion(bf16[2,8192,128]{2,1,0:T(8,128)(2,1)} %param.13, s32[]{:T(128)S(6)} %select_n.79, s32[]{:T(128)S(6)} %select_n.75, s32[]{:T(128)S(6)} %select_n.73, s32[]{:T(128)S(6)} %select_n.77), kind=kLoop, calls=%fused_computation.12 | loop fusion | bytes 4194320 | tf_op jit(solution)/shard_map/dynamic_slice | solution.py:388
  11.2 2.4 %collective-permute-start.10 = (bf16[2,1024,128]{2,1,0:T(8,128)(2,1)}, bf16[2,1024,128]{2,1,0:T(8,128)(2,1)}, u32[]{:S(2)}, u32[]{:S(2)}) collective-permute-start(bf16[2,1024,128]{2,1,0:T(8,128)(2,1)} %get-tuple-element.25), channel_id=1, source_target_pairs={{0,0},{8,1},{16,16},{24,17},{32,32},{40,33},{48,48},{56,49},{64,64... | collective-permute-start | bytes 1572872 | tf_op jit(solution)/shard_map/ppermute | solution.py:53
  13.6 2.6 %collective-permute-start.7 = (bf16[2,1024,128]{2,1,0:T(8,128)(2,1)}, bf16[2,1024,128]{2,1,0:T(8,128)(2,1)}, u32[]{:S(2)}, u32[]{:S(2)}) collective-permute-start(bf16[2,1024,128]{2,1,0:T(8,128)(2,1)} %get-tuple-element.28), channel_id=1, source_target_pairs={{0,6},{8,7},{16,22},{24,23},{32,38},{40,39},{48,54},{56,55},{64,70... | collective-permute-start | bytes 1572872 | tf_op jit(solution)/shard_map/ppermute | solution.py:53
  16.2 0.5 collective-permute-start.4
  16.7 2.4 %collective-permute-start.1 = (bf16[2,1024,128]{2,1,0:T(8,128)(2,1)}, bf16[2,1024,128]{2,1,0:T(8,128)(2,1)S(1)}, u32[]{:S(2)}, u32[]{:S(2)}) collective-permute-start(bf16[2,1024,128]{2,1,0:T(8,128)(2,1)} %get-tuple-element.27), channel_id=1, source_target_pairs={{0,4},{8,5},{16,20},{24,21},{32,36},{40,37},{48,52},{56,53},{64,68... | collective-permute-start | bytes 1572872 | tf_op jit(solution)/shard_map/ppermute | solution.py:53
  19.1 0.7 dynamic_slice.15
  19.8 0.2 convert_reduce_fusion
  20.0 5.4 %prepare.1 = (bf16[1024,1024]{1,0:T(8,128)(2,1)S(1)}, bf16[1024,1024]{1,0:T(8,128)(2,1)S(1)}, f32[16,256]{1,0:T(8,128)S(1)}, f32[16,256]{1,0:T(8,128)S(1)}) custom-call(s32[1]{0:T(128)} %bitcast.2.own_slot, bf16[1024,1024]{1,0:T(8,128)(2,1)S(1)} %copy-done, bf16[1024,1024]{1,0:T(8,128)(2,1)} %collective-permute-done.other, f32[1,1024]{1,0:T(1,128)S(1)} %bitcast.5), custom_call_target="tpu_custom_call" | custom-call | flops 16777216 | bytes 8388608 | tf_op jit(solution)/shard_map/prepare/pallas_call | solution.py:101
  25.3 10.9 %collective-permute-done.10.weight = bf16[2,1024,128]{2,1,0:T(8,128)(2,1)} collective-permute-done((bf16[2,1024,128]{2,1,0:T(8,128)(2,1)}, bf16[2,1024,128]{2,1,0:T(8,128)(2,1)}, u32[]{:S(2)}, u32[]{:S(2)}) %collective-permute-start.10) | collective-permute-done | bytes 524320 | tf_op jit(solution)/shard_map/ppermute | solution.py:53
  36.3 2.3 %project.15 = bf16[1040,256]{1,0:T(8,128)(2,1)S(1)} custom-call(bf16[1024,1024]{1,0:T(8,128)(2,1)S(1)} %get-tuple-element.16.tokens, f32[16,256]{1,0:T(8,128)S(1)} %get-tuple-element.17.squares, bf16[2,1024,128]{2,1,0:T(8,128)(2,1)} %collective-permute-done.10.weight), custom_call_target="tpu_custom_call" | custom-call | flops 536870912 | bytes 3145728 | tf_op jit(solution)/shard_map/project/pallas_call | solution.py:130
  38.6 0.1 collective-permute-start.12
  38.7 2.3 %project.14 = bf16[1040,256]{1,0:T(8,128)(2,1)S(1)} custom-call(bf16[1024,1024]{1,0:T(8,128)(2,1)S(1)} %get-tuple-element.14.tokens, f32[16,256]{1,0:T(8,128)S(1)} %get-tuple-element.15.squares, bf16[2,1024,128]{2,1,0:T(8,128)(2,1)} %collective-permute-done.10.weight), custom_call_target="tpu_custom_call" | custom-call | flops 536870912 | bytes 3145728 | tf_op jit(solution)/shard_map/project/pallas_call | solution.py:130
  41.0 3.2 %collective-permute-start.11 = (bf16[1040,256]{1,0:T(8,128)(2,1)S(1)}, bf16[1040,256]{1,0:T(8,128)(2,1)S(1)}, u32[]{:S(2)}, u32[]{:S(2)}) collective-permute-start(bf16[1040,256]{1,0:T(8,128)(2,1)S(1)} %project.14), channel_id=1, source_target_pairs={{0,0},{8,1},{16,16},{24,17},{32,32},{40,33},{48,48},{56,49},{64,64... | collective-permute-start | bytes 1597448 | tf_op jit(solution)/shard_map/ppermute | solution.py:53
  44.3 2.3 %project.13 = bf16[1040,256]{1,0:T(8,128)(2,1)S(1)} custom-call(bf16[1024,1024]{1,0:T(8,128)(2,1)S(1)} %get-tuple-element.16.tokens, f32[16,256]{1,0:T(8,128)S(1)} %get-tuple-element.17.squares, bf16[2,1024,128]{2,1,0:T(8,128)(2,1)} %collective-permute-done.7.weight), custom_call_target="tpu_custom_call" | custom-call | flops 536870912 | bytes 3145728 | tf_op jit(solution)/shard_map/project/pallas_call | solution.py:130
  46.6 0.1 collective-permute-start.9
  46.7 0.1 add_convert_fusion
  46.8 2.3 %project.12 = bf16[1040,256]{1,0:T(8,128)(2,1)S(1)} custom-call(bf16[1024,1024]{1,0:T(8,128)(2,1)S(1)} %get-tuple-element.14.tokens, f32[16,256]{1,0:T(8,128)S(1)} %get-tuple-element.15.squares, bf16[2,1024,128]{2,1,0:T(8,128)(2,1)} %collective-permute-done.7.weight), custom_call_target="tpu_custom_call" | custom-call | flops 536870912 | bytes 3145728 | tf_op jit(solution)/shard_map/project/pallas_call | solution.py:130
  49.1 3.4 %collective-permute-start.8 = (bf16[1040,256]{1,0:T(8,128)(2,1)S(1)}, bf16[1040,256]{1,0:T(8,128)(2,1)}, u32[]{:S(2)}, u32[]{:S(2)}) collective-permute-start(bf16[1040,256]{1,0:T(8,128)(2,1)S(1)} %project.12), channel_id=1, source_target_pairs={{0,2},{8,3},{16,18},{24,19},{32,34},{40,35},{48,50},{56,51},{64,66... | collective-permute-start | bytes 1597448 | tf_op jit(solution)/shard_map/ppermute | solution.py:53
  52.6 2.1 %project.11 = bf16[1040,256]{1,0:T(8,128)(2,1)} custom-call(bf16[1024,1024]{1,0:T(8,128)(2,1)S(1)} %get-tuple-element.16.tokens, f32[16,256]{1,0:T(8,128)S(1)} %get-tuple-element.17.squares, bf16[2,1024,128]{2,1,0:T(8,128)(2,1)S(1)} %collective-permute-done.4.weight), custom_call_target="tpu_custom_call" | custom-call | flops 536870912 | bytes 3145728 | tf_op jit(solution)/shard_map/project/pallas_call | solution.py:130
  54.6 2.1 %project.10 = bf16[1040,256]{1,0:T(8,128)(2,1)} custom-call(bf16[1024,1024]{1,0:T(8,128)(2,1)S(1)} %get-tuple-element.14.tokens, f32[16,256]{1,0:T(8,128)S(1)} %get-tuple-element.15.squares, bf16[2,1024,128]{2,1,0:T(8,128)(2,1)S(1)} %collective-permute-done.4.weight), custom_call_target="tpu_custom_call" | custom-call | flops 536870912 | bytes 3145728 | tf_op jit(solution)/shard_map/project/pallas_call | solution.py:130
  56.7 3.2 %collective-permute-start.6 = (bf16[1040,256]{1,0:T(8,128)(2,1)}, bf16[1040,256]{1,0:T(8,128)(2,1)}, u32[]{:S(2)}, u32[]{:S(2)}) collective-permute-start(bf16[1040,256]{1,0:T(8,128)(2,1)} %project.11), channel_id=1, source_target_pairs={{0,14},{8,15},{16,30},{24,31},{32,46},{40,47},{48,62},{56,63},{64,... | collective-permute-start | bytes 1597448 | tf_op jit(solution)/shard_map/ppermute | solution.py:53
  59.9 2.1 %project.9 = bf16[1040,256]{1,0:T(8,128)(2,1)} custom-call(bf16[1024,1024]{1,0:T(8,128)(2,1)S(1)} %get-tuple-element.16.tokens, f32[16,256]{1,0:T(8,128)S(1)} %get-tuple-element.17.squares, bf16[2,1024,128]{2,1,0:T(8,128)(2,1)S(1)} %collective-permute-done.1.weight), custom_call_target="tpu_custom_call" | custom-call | flops 536870912 | bytes 3145728 | tf_op jit(solution)/shard_map/project/pallas_call | solution.py:130
  62.0 1.2 project.8
  63.2 0.8 copy-done.4
  64.1 0.8 copy-done.6
  64.8 1.8 %collective-permute-start.3 = (bf16[1040,256]{1,0:T(8,128)(2,1)}, bf16[1040,256]{1,0:T(8,128)(2,1)}, u32[]{:S(2)}, u32[]{:S(2)}) collective-permute-start(bf16[1040,256]{1,0:T(8,128)(2,1)} %project.9), channel_id=1, source_target_pairs={{0,12},{8,13},{16,28},{24,29},{32,44},{40,45},{48,60},{56,61},{64,... | collective-permute-start | bytes 1597448 | tf_op jit(solution)/shard_map/ppermute | solution.py:53
  66.7 0.8 copy-done.8
  67.5 2.2 %collective-permute-start.2 = (bf16[1040,256]{1,0:T(8,128)(2,1)S(1)}, bf16[1040,256]{1,0:T(8,128)(2,1)}, u32[]{:S(2)}, u32[]{:S(2)}) collective-permute-start(bf16[1040,256]{1,0:T(8,128)(2,1)S(1)} %project.8), channel_id=1, source_target_pairs={{0,4},{8,5},{16,20},{24,21},{32,36},{40,37},{48,52},{56,53},{64,68... | collective-permute-start | bytes 1597448 | tf_op jit(solution)/shard_map/ppermute | solution.py:53
  69.6 0.1 convert_element_type.18
  69.8 0.1 select_reduce_fusion
  69.9 1.9 %fusion = (f32[1024,64]{1,0:T(8,128)S(1)}, f32[1024,64]{1,0:T(8,128)S(1)}, f32[1024,64]{1,0:T(8,128)S(1)}) fusion(f32[64]{0:T(128)S(1)} %multiply_exponential_fusion, f32[1024]{0:T(1024)S(1)} %convert_element_type.18), kind=kLoop, calls=%fused_computation.4 | loop fusion | flops 131072 | bytes 790784 | tf_op jit(solution)/shard_map/neg | solution.py:349
  71.8 0.3 pad_maximum_fusion
  72.2 45.6 %all-gather.2.cloned.1.call-done.refs_11_ = bf16[32,128,128]{2,1,0:T(8,128)(2,1)} async-done(((bf16[1,128,128]{2,1,0:T(8,128)(2,1)}), bf16[32,128,128]{2,1,0:T(8,128)(2,1)}) %all-gather.2.cloned.1.call-update) | async-done | bytes 1048592 | tf_op jit(solution)/shard_map/all_gather | solution.py:381
  117.8 1.2 copy-done.3
  119.0 1.0 copy-done.7
  120.1 1.0 copy-done.9
  121.1 9.6 %finish.1 = (bf16[16,144,128]{2,1,0:T(8,128)(2,1)S(1)}, bf16[16,144,128]{2,1,0:T(8,128)(2,1)S(1)}) custom-call(s32[256]{0:T(256)S(1)} %get-tuple-element.24.pages, s32[256]{0:T(256)S(1)} %get-tuple-element.23.page_rows, s32[1]{0:T(128)} %bitcast.1.core, bf16[1040,256]{1,0:T(8,128)(2,1)} %collective-permute-done.2.refs_0_, ...), custom_call_target="tpu_custom_call" | custom-call | flops 134217728 | bytes 16777216 | tf_op jit(solution)/shard_map/finish/pallas_call | solution.py:266
  130.7 0.3 collective-permute-start.13
  131.1 1.7 %collective-permute-done.13.right = bf16[16,144,128]{2,1,0:T(8,128)(2,1)S(1)} collective-permute-done((bf16[16,144,128]{2,1,0:T(8,128)(2,1)S(1)}, bf16[16,144,128]{2,1,0:T(8,128)(2,1)S(1)}, u32[]{:S(2)}, u32[]{:S(2)}) %collective-permute-start.13) | collective-permute-done | bytes 589856 | tf_op jit(solution)/shard_map/ppermute | solution.py:53
  132.8 1.2 merge.1
  134.0 4.4 %all-to-all-start = ((bf16[16,144,128]{2,1,0:T(8,128)(2,1)}), bf16[16,144,128]{2,1,0:T(8,128)(2,1)S(1)}, u32[]{:S(2)}, u32[]{:S(2)}) async-start(bf16[16,144,128]{2,1,0:T(8,128)(2,1)} %merge.1), calls=%async_computation | async-start | bytes 1179648 | tf_op jit(solution)/shard_map/all_to_all | solution.py:414
  138.5 1.6 copy-done.2
  140.1 6.5 %resident.1 = (f32[128,128]{1,0:T(8,128)S(1)}, f32[8,128]{1,0:T(8,128)S(1)}, f32[8,128]{1,0:T(8,128)S(1)}) custom-call(s32[16]{0:T(128)S(1)} %copy-done.10, bf16[128,128]{1,0:T(8,128)(2,1)S(1)} %reshape.45.queries, bf16[16,512,128]{2,1,0:T(8,128)(2,1)S(1)} %copy-done.1, bf16[16,512,128]{2,1,0:T(8,128)(2,1)S(1)} %copy-done.2), custom_call_target="tpu_custom_call" | custom-call | flops 33554432 | bytes 16777216 | tf_op jit(solution)/shard_map/resident/pallas_call | solution.py:171
  146.6 12.8 %all-to-all-done.received = bf16[16,144,128]{2,1,0:T(8,128)(2,1)S(1)} async-done(((bf16[16,144,128]{2,1,0:T(8,128)(2,1)}), bf16[16,144,128]{2,1,0:T(8,128)(2,1)S(1)}, u32[]{:S(2)}, u32[]{:S(2)}) %all-to-all-start) | async-done | bytes 589856 | tf_op jit(solution)/shard_map/all_to_all | solution.py:414
  159.4 0.9 conclude.1
  (43 shorter events, 0.1 us)
Async XLA Ops:
  6.5 111.2 %all-gather.2.cloned.1.call-start = ((), (), s32[]{:S(2)}) async-start(), calls=%async_computation.1 | async-start | bytes 1081344 | tf_op jit(solution)/shard_map/all_gather | solution.py:381
  6.5 13.4 %collective-permute-start = (bf16[1024,1024]{1,0:T(8,128)(2,1)}, bf16[1024,1024]{1,0:T(8,128)(2,1)}, u32[]{:S(2)}, u32[]{:S(2)}) collective-permute-start(bf16[1024,1024]{1,0:T(8,128)(2,1)} %own.1), channel_id=1, source_target_pairs={{0,8},{8,0},{16,24},{24,16},{32,40},{40,32},{48,56},{56,48},{64,72... | collective-permute-start | bytes 6291464 | tf_op jit(solution)/shard_map/ppermute | solution.py:53
  8.1 11.7 %copy-start.14 = (s32[128,1]{0,1:T(1,128)S(1)}, s32[128,1]{0,1:T(1,128)}, u32[]{:S(2)}) copy-start(s32[128,1]{0,1:T(1,128)} %param.15) | copy-start | bytes 1540
  8.1 11.9 %copy-start = (bf16[1024,1024]{1,0:T(8,128)(2,1)S(1)}, bf16[1024,1024]{1,0:T(8,128)(2,1)}, u32[]{:S(2)}) copy-start(bf16[1024,1024]{1,0:T(8,128)(2,1)} %own.1) | copy-start | bytes 6291460
  11.2 25.1 %collective-permute-start.10 = (bf16[2,1024,128]{2,1,0:T(8,128)(2,1)}, bf16[2,1024,128]{2,1,0:T(8,128)(2,1)}, u32[]{:S(2)}, u32[]{:S(2)}) collective-permute-start(bf16[2,1024,128]{2,1,0:T(8,128)(2,1)} %get-tuple-element.25), channel_id=1, source_target_pairs={{0,0},{8,1},{16,16},{24,17},{32,32},{40,33},{48,48},{56,49},{64,64... | collective-permute-start | bytes 1572872 | tf_op jit(solution)/shard_map/ppermute | solution.py:53
  13.6 30.7 %collective-permute-start.7 = (bf16[2,1024,128]{2,1,0:T(8,128)(2,1)}, bf16[2,1024,128]{2,1,0:T(8,128)(2,1)}, u32[]{:S(2)}, u32[]{:S(2)}) collective-permute-start(bf16[2,1024,128]{2,1,0:T(8,128)(2,1)} %get-tuple-element.28), channel_id=1, source_target_pairs={{0,6},{8,7},{16,22},{24,23},{32,38},{40,39},{48,54},{56,55},{64,70... | collective-permute-start | bytes 1572872 | tf_op jit(solution)/shard_map/ppermute | solution.py:53
  16.2 32.9 %collective-permute-start.4 = (bf16[2,1024,128]{2,1,0:T(8,128)(2,1)}, bf16[2,1024,128]{2,1,0:T(8,128)(2,1)S(1)}, u32[]{:S(2)}, u32[]{:S(2)}) collective-permute-start(bf16[2,1024,128]{2,1,0:T(8,128)(2,1)} %get-tuple-element.26), channel_id=1, source_target_pairs={{0,2},{8,3},{16,18},{24,19},{32,34},{40,35},{48,50},{56,51},{64,66... | collective-permute-start | bytes 1572872 | tf_op jit(solution)/shard_map/ppermute | solution.py:53
  16.7 40.0 %collective-permute-start.1 = (bf16[2,1024,128]{2,1,0:T(8,128)(2,1)}, bf16[2,1024,128]{2,1,0:T(8,128)(2,1)S(1)}, u32[]{:S(2)}, u32[]{:S(2)}) collective-permute-start(bf16[2,1024,128]{2,1,0:T(8,128)(2,1)} %get-tuple-element.27), channel_id=1, source_target_pairs={{0,4},{8,5},{16,20},{24,21},{32,36},{40,37},{48,52},{56,53},{64,68... | collective-permute-start | bytes 1572872 | tf_op jit(solution)/shard_map/ppermute | solution.py:53
  38.6 24.6 %collective-permute-start.12 = (bf16[1040,256]{1,0:T(8,128)(2,1)S(1)}, bf16[1040,256]{1,0:T(8,128)(2,1)S(1)}, u32[]{:S(2)}, u32[]{:S(2)}) collective-permute-start(bf16[1040,256]{1,0:T(8,128)(2,1)S(1)} %project.15), channel_id=1, source_target_pairs={{0,8},{8,9},{16,24},{24,25},{32,40},{40,41},{48,56},{56,57},{64,72... | collective-permute-start | bytes 1597448 | tf_op jit(solution)/shard_map/ppermute | solution.py:53
  41.0 5.7 %copy-start.12 = (s32[128]{0:T(128)S(1)}, s32[128]{0:T(128)}, u32[]{:S(2)}) copy-start(s32[128]{0:T(128)} %param.17) | copy-start | bytes 1540
  41.0 23.0 %collective-permute-start.11 = (bf16[1040,256]{1,0:T(8,128)(2,1)S(1)}, bf16[1040,256]{1,0:T(8,128)(2,1)S(1)}, u32[]{:S(2)}, u32[]{:S(2)}) collective-permute-start(bf16[1040,256]{1,0:T(8,128)(2,1)S(1)} %project.14), channel_id=1, source_target_pairs={{0,0},{8,1},{16,16},{24,17},{32,32},{40,33},{48,48},{56,49},{64,64... | collective-permute-start | bytes 1597448 | tf_op jit(solution)/shard_map/ppermute | solution.py:53
  46.6 20.1 %collective-permute-start.9 = (bf16[1040,256]{1,0:T(8,128)(2,1)S(1)}, bf16[1040,256]{1,0:T(8,128)(2,1)S(1)}, u32[]{:S(2)}, u32[]{:S(2)}) collective-permute-start(bf16[1040,256]{1,0:T(8,128)(2,1)S(1)} %project.13), channel_id=1, source_target_pairs={{0,10},{8,11},{16,26},{24,27},{32,42},{40,43},{48,58},{56,59},{64,... | collective-permute-start | bytes 1597448 | tf_op jit(solution)/shard_map/ppermute | solution.py:53
  49.1 68.6 %collective-permute-start.8 = (bf16[1040,256]{1,0:T(8,128)(2,1)S(1)}, bf16[1040,256]{1,0:T(8,128)(2,1)}, u32[]{:S(2)}, u32[]{:S(2)}) collective-permute-start(bf16[1040,256]{1,0:T(8,128)(2,1)S(1)} %project.12), channel_id=1, source_target_pairs={{0,2},{8,3},{16,18},{24,19},{32,34},{40,35},{48,50},{56,51},{64,66... | collective-permute-start | bytes 1597448 | tf_op jit(solution)/shard_map/ppermute | solution.py:53
  56.7 61.1 %collective-permute-start.6 = (bf16[1040,256]{1,0:T(8,128)(2,1)}, bf16[1040,256]{1,0:T(8,128)(2,1)}, u32[]{:S(2)}, u32[]{:S(2)}) collective-permute-start(bf16[1040,256]{1,0:T(8,128)(2,1)} %project.11), channel_id=1, source_target_pairs={{0,14},{8,15},{16,30},{24,31},{32,46},{40,47},{48,62},{56,63},{64,... | collective-permute-start | bytes 1597448 | tf_op jit(solution)/shard_map/ppermute | solution.py:53
  62.0 7.8 %copy-start.15 = (bf16[2,128]{1,0:T(2,128)(2,1)S(1)}, bf16[2,128]{1,0:T(2,128)(2,1)}, u32[]{:S(2)}) copy-start(bf16[2,128]{1,0:T(2,128)(2,1)} %param.14) | copy-start | bytes 1540
  62.0 7.8 %copy-start.13 = (s32[128]{0:T(128)S(1)}, s32[128]{0:T(128)}, u32[]{:S(2)}) copy-start(s32[128]{0:T(128)} %param.16) | copy-start | bytes 1540
  63.2 0.8 copy-start.4
  64.0 53.7 %collective-permute-start.5 = (bf16[1040,256]{1,0:T(8,128)(2,1)}, bf16[1040,256]{1,0:T(8,128)(2,1)}, u32[]{:S(2)}, u32[]{:S(2)}) collective-permute-start(bf16[1040,256]{1,0:T(8,128)(2,1)} %project.10), channel_id=1, source_target_pairs={{0,6},{8,7},{16,22},{24,23},{32,38},{40,39},{48,54},{56,55},{64,70... | collective-permute-start | bytes 1597448 | tf_op jit(solution)/shard_map/ppermute | solution.py:53
  64.0 0.8 copy-start.6
  64.8 52.9 %collective-permute-start.3 = (bf16[1040,256]{1,0:T(8,128)(2,1)}, bf16[1040,256]{1,0:T(8,128)(2,1)}, u32[]{:S(2)}, u32[]{:S(2)}) collective-permute-start(bf16[1040,256]{1,0:T(8,128)(2,1)} %project.9), channel_id=1, source_target_pairs={{0,12},{8,13},{16,28},{24,29},{32,44},{40,45},{48,60},{56,61},{64,... | collective-permute-start | bytes 1597448 | tf_op jit(solution)/shard_map/ppermute | solution.py:53
  66.7 0.8 copy-start.8
  67.5 50.3 %collective-permute-start.2 = (bf16[1040,256]{1,0:T(8,128)(2,1)S(1)}, bf16[1040,256]{1,0:T(8,128)(2,1)}, u32[]{:S(2)}, u32[]{:S(2)}) collective-permute-start(bf16[1040,256]{1,0:T(8,128)(2,1)S(1)} %project.8), channel_id=1, source_target_pairs={{0,4},{8,5},{16,20},{24,21},{32,36},{40,37},{48,52},{56,53},{64,68... | collective-permute-start | bytes 1597448 | tf_op jit(solution)/shard_map/ppermute | solution.py:53
  69.9 47.9 %copy-start.5 = (bf16[1040,256]{1,0:T(8,128)(2,1)S(1)}, bf16[1040,256]{1,0:T(8,128)(2,1)}, u32[]{:S(2)}) copy-start(bf16[1040,256]{1,0:T(8,128)(2,1)} %copy-done.4) | copy-start | bytes 1597444
  117.8 1.2 copy-start.3
  119.0 1.0 copy-start.7
  120.1 1.0 copy-start.9
  130.7 7.7 %copy-start.11 = (bf16[16,1024]{1,0:T(8,128)(2,1)S(1)}, bf16[16,1024]{1,0:T(8,128)(2,1)}, u32[]{:S(2)}) copy-start(bf16[16,1024]{1,0:T(8,128)(2,1)} %param.18) | copy-start | bytes 98308
  130.7 7.7 %copy-start.1 = (bf16[16,512,128]{2,1,0:T(8,128)(2,1)S(1)}, bf16[16,512,128]{2,1,0:T(8,128)(2,1)}, u32[]{:S(2)}) copy-start(bf16[16,512,128]{2,1,0:T(8,128)(2,1)} %keys.1) | copy-start | bytes 6291460
  130.7 7.7 %copy-start.10 = (s32[16]{0:T(128)S(1)}, s32[16]{0:T(128)}, u32[]{:S(2)}) copy-start(s32[16]{0:T(128)} %lengths.1) | copy-start | bytes 196
  130.7 2.1 %collective-permute-start.13 = (bf16[16,144,128]{2,1,0:T(8,128)(2,1)S(1)}, bf16[16,144,128]{2,1,0:T(8,128)(2,1)S(1)}, u32[]{:S(2)}, u32[]{:S(2)}) collective-permute-start(bf16[16,144,128]{2,1,0:T(8,128)(2,1)S(1)} %get-tuple-element.19), channel_id=1, source_target_pairs={{0,8},{8,0},{16,24},{24,16},{32,40},{40,32},{48,56},{56,48},{64,72... | collective-permute-start | bytes 1769480 | tf_op jit(solution)/shard_map/ppermute | solution.py:53
  134.0 25.4 %all-to-all-start = ((bf16[16,144,128]{2,1,0:T(8,128)(2,1)}), bf16[16,144,128]{2,1,0:T(8,128)(2,1)S(1)}, u32[]{:S(2)}, u32[]{:S(2)}) async-start(bf16[16,144,128]{2,1,0:T(8,128)(2,1)} %merge.1), calls=%async_computation | async-start | bytes 1179648 | tf_op jit(solution)/shard_map/all_to_all | solution.py:414
  138.5 1.6 copy-start.2
Sparse Core Ops, SparseCore 0:
  10.1 107.5 all-gather.1

commit v2 on v1

--- a/solution.py
+++ b/solution.py
@@ -17,7 +17,9 @@
 ROWS = 16
 GROUPS = 8
 CONTEXT = 512
-TILE = 256
+TILE = 128
+CHUNKS = (640, 384)
+STEP = 32
 STAT = 16
 LOW = -1e30
 MIB = 1 << 20
@@ -27,6 +29,7 @@
 BF16 = jnp.bfloat16
 VMEM = pl.BlockSpec(memory_space=pltpu.VMEM)
 SMEM = pl.BlockSpec(memory_space=pltpu.SMEM)
+HBM = pl.BlockSpec(memory_space=pltpu.HBM)
 
 
 def cost(flops, bytes_accessed):
@@ -53,94 +56,97 @@
     return lax.ppermute(array, ("rep", "tp"), pairs)
 
 
-def prepare_kernel(own_slot, own, other, gain, first, second, squares_first, squares_second):
-    tile = pl.program_id(0)
-    ones = jnp.ones((8, FEAT), BF16)
-
-    def scaled(ref):
-        values = ref[...].astype(F32)
-        return (values * gain[...]).astype(BF16)
-
-    def squares(ref):
-        values = ref[...].astype(F32)
-        square = values * values
-        high = square.astype(BF16)
-        low = (square - high.astype(F32)).astype(BF16)
-        total = lax.dot_general(ones, high, NT, preferred_element_type=F32)
-        total = total + lax.dot_general(ones, low, NT, preferred_element_type=F32)
-        total = total[0:1, :]
-        top = total.astype(BF16).astype(F32)
-        rest = (total - top).astype(BF16).astype(F32)
-        return top, rest
-
-    def write(source_a, source_b):
-        first[...] = scaled(source_a)
-        second[...] = scaled(source_b)
-        for source, out in ((source_a, squares_first), (source_b, squares_second)):
-            top, rest = squares(source)
-            out[pl.ds(tile, 1), :] = top
-            out[pl.ds(tile + 4, 1), :] = rest
-
-    @pl.when(tile == 0)
-    def _():
-        squares_first[...] = jnp.zeros_like(squares_first)
-        squares_second[...] = jnp.zeros_like(squares_second)
-
-    @pl.when(own_slot[0] == 0)
-    def _():
-        write(own, other)
-
-    @pl.when(own_slot[0] != 0)
-    def _():
-        write(other, own)
-
-
-def prepare(own_slot, own, other, gain):
-    tokens = pl.BlockSpec((TILE, FEAT), lambda i: (i, 0))
-    squares = pl.BlockSpec((STAT, TILE), lambda i: (0, 0))
+def after(value, other):
+    if other is None:
+        return value
+    return lax.optimization_barrier((value, other))[0]
+
+
+def project_kernel(start, same, own, other, own_gain, other_gain, *refs):
+    weights, outs = refs[0:8], refs[8:12]
+    tokens_store, scaled, folded, store, results, arrived, left = refs[12:]
+    count = other.shape[0]
+    copies = [
+        pltpu.make_async_copy(own.at[pl.ds(start, count), :], tokens_store.at[0], arrived.at[8]),
+        pltpu.make_async_copy(other, tokens_store.at[1], arrived.at[9]),
+    ]
+    for head in (2, 1, 3, 0):
+        for i in (head, head + 4):
+            copies.append(pltpu.make_async_copy(weights[i], store.at[i], arrived.at[i]))
+    for copy in copies[:4]:
+        copy.start()
+    ones = jnp.ones((8, TILE), BF16)
+
+    copies[0].wait()
+    copies[1].wait()
+    for copy in copies[4:]:
+        copy.start()
+
+    def scale(step, carry):
+        rows = pl.ds(pl.multiple_of(step * STEP, STEP), STEP)
+        own_values, other_values = (tokens_store[i, rows, :].astype(F32) for i in (0, 1))
+        square = own_values * own_values + other_values * other_values
+        sums = square[:, 0:TILE]
+        for part in range(1, FEAT // TILE):
+            sums = sums + square[:, part * TILE : (part + 1) * TILE]
+        folded[rows, :] = sums
+        scaled[1 - same[0], rows, :] = (own_values * own_gain[...]).astype(BF16)
+        scaled[same[0], rows, :] = (other_values * other_gain[...]).astype(BF16)
+        return carry
+
+    lax.fori_loop(0, count // STEP, scale, 0)
+    high = folded[...].astype(BF16)
+    low = (folded[...] - high.astype(F32)).astype(BF16)
+    total = lax.dot_general(ones, high, NT, preferred_element_type=F32)
+    total = (total + lax.dot_general(ones, low, NT, preferred_element_type=F32))[0:1, :]
+    top = total.astype(BF16).astype(F32)
+    rest = total - top
+    index = lax.broadcasted_iota(jnp.int32, (STAT, TILE), 0)
+    table = jnp.zeros((STAT, TILE), F32)
+    for tile in range(count // TILE):
+        token = slice(tile * TILE, (tile + 1) * TILE)
+        table = jnp.where(index == tile, top[:, token], table)
+        table = jnp.where(index == tile + 8, rest[:, token], table)
+    table = jnp.concatenate([table, jnp.zeros_like(table)], axis=1).astype(BF16)
+
+    leaving = []
+    for number, head in enumerate((2, 1, 3, 0)):
+        copies[2 + 2 * number].wait()
+        copies[3 + 2 * number].wait()
+        near = jnp.concatenate([store[head, 0], store[head, 1]], axis=1)
+        far = jnp.concatenate([store[head + 4, 0], store[head + 4, 1]], axis=1)
+        for tile in range(0, count, TILE):
+            rows = slice(tile, tile + TILE)
+            part = jnp.dot(scaled[0, rows, :], near, preferred_element_type=F32)
+            part = part + jnp.dot(scaled[1, rows, :], far, preferred_element_type=F32)
+            results[head, rows, :] = part.astype(BF16)
+        results[head, count:, :] = table
+        leaving.append(pltpu.make_async_copy(results.at[head], outs[head], left.at[head]))
+        leaving[-1].start()
+    for copy in leaving:
+        copy.wait()
+
+
+def project(same, prompt, start, other, own_gain, other_gain, near, far):
+    count = other.shape[0]
     return pl.pallas_call(
-        prepare_kernel,
-        grid=(TOK // TILE,),
-        in_specs=[SMEM, tokens, tokens, pl.BlockSpec((1, FEAT), lambda i: (0, 0))],
-        out_specs=[tokens, tokens, squares, squares],
-        out_shape=[
-            jax.ShapeDtypeStruct((TOK, FEAT), BF16),
-            jax.ShapeDtypeStruct((TOK, FEAT), BF16),
-            jax.ShapeDtypeStruct((STAT, TILE), F32),
-            jax.ShapeDtypeStruct((STAT, TILE), F32),
+        functools.partial(project_kernel, start),
+        in_specs=[SMEM, HBM, HBM, VMEM, VMEM] + [HBM] * 8,
+        out_specs=[HBM] * 4,
+        out_shape=[jax.ShapeDtypeStruct((count + STAT, 2 * HEAD_DIM), BF16)] * 4,
+        scratch_shapes=[
+            pltpu.VMEM((2, count, FEAT), BF16),
+            pltpu.VMEM((2, count, FEAT), BF16),
+            pltpu.VMEM((count, TILE), F32),
+            pltpu.VMEM((8, 2, FEAT, HEAD_DIM), BF16),
+            pltpu.VMEM((4, count + STAT, 2 * HEAD_DIM), BF16),
+            pltpu.SemaphoreType.DMA((10,)),
+            pltpu.SemaphoreType.DMA((4,)),
         ],
-        compiler_params=params(24),
-        cost_estimate=cost(16 * TOK * FEAT, 8 * MIB),
-        name="prepare",
-    )(own_slot, own, other, gain)
-
-
-def project_kernel(tokens, squares, weight, out):
-    tile = pl.program_id(0)
-    both = jnp.concatenate([weight[0], weight[1]], axis=1)
-    part = lax.dot_general(tokens[...], both, (((1,), (0,)), ((), ())), preferred_element_type=F32)
-    out[pl.ds(pl.multiple_of(tile * TILE, TILE), TILE), :] = part.astype(BF16)
-
-    @pl.when(tile == 0)
-    def _():
-        out[TOK : TOK + STAT, :] = squares[...].astype(BF16)
-
-
-def project(tokens, squares, weight):
-    return pl.pallas_call(
-        project_kernel,
-        grid=(TOK // TILE,),
-        in_specs=[
-            pl.BlockSpec((TILE, FEAT), lambda i: (i, 0)),
-            pl.BlockSpec((STAT, TILE), lambda i: (0, 0)),
-            pl.BlockSpec((2, FEAT, HEAD_DIM), lambda i: (0, 0, 0)),
-        ],
-        out_specs=pl.BlockSpec((TOK + STAT, 2 * HEAD_DIM), lambda i: (0, 0)),
-        out_shape=jax.ShapeDtypeStruct((TOK + STAT, 2 * HEAD_DIM), BF16),
-        compiler_params=params(16),
-        cost_estimate=cost(2 * TOK * FEAT * 2 * HEAD_DIM, 3 * MIB),
+        compiler_params=params(40),
+        cost_estimate=cost(2 * count * 2 * FEAT * 8 * HEAD_DIM, 6 * MIB),
         name="project",
-    )(tokens, squares, weight)
+    )(same, prompt, other, own_gain, other_gain, *near, *far)
 
 
 def resident_kernel(lengths, queries, keys, values, out, top_out, total_out, sums, tops, totals):
@@ -205,14 +211,15 @@
     return top, stats[3:4] + stats[4:5]
 
 
-def finish_kernel(pages, page_rows, core, *refs):
-    parts = refs[:8]
-    cosine, sine, bias, queries, kept, sent, key_store, value_store = refs[8:]
-    squares = jnp.concatenate([part[TOK : TOK + STAT, :] for part in parts], axis=0)
-    index = lax.broadcasted_iota(jnp.int32, (8 * STAT, HEAD_DIM), 0)
-    for tile in range(TOK // TILE):
+def finish_chunk(parts, cosine, sine, bias, start, key_out, value_out, place):
+    count = parts[0].shape[0] - STAT
+    squares = jnp.concatenate([part[count:, 0:TILE] for part in parts], axis=0)
+    index = lax.broadcasted_iota(jnp.int32, (len(parts) * STAT, HEAD_DIM), 0)
+    for tile in range(count // TILE):
         token = slice(tile * TILE, (tile + 1) * TILE)
-        chosen = ((index % STAT) < 8) & ((index % 4) == tile)
+        table = slice(start + tile * TILE, start + (tile + 1) * TILE)
+        target = slice(place + tile * TILE, place + (tile + 1) * TILE)
+        chosen = (index % 8) == tile
         total = lax.dot_general(
             squares, jnp.where(chosen, 1.0, 0.0).astype(BF16), TN, preferred_element_type=F32
         )
@@ -222,13 +229,42 @@
             added = added + part[token, :].astype(F32)
         keys = added[:, :HEAD_DIM] * inverse + bias[0:1, :]
         values = added[:, HEAD_DIM:] * inverse + bias[1:2, :]
-        keys = keys * cosine[token, :] + pltpu.roll(keys, HEAD_DIM // 2, 1) * sine[token, :]
-        key_store[token, :] = keys.astype(BF16).astype(F32)
-        value_store[token, :] = values.astype(BF16).astype(F32)
-
+        keys = keys * cosine[table, :] + pltpu.roll(keys, HEAD_DIM // 2, 1) * sine[table, :]
+        key_out[target, :] = keys.astype(BF16).astype(F32)
+        value_out[target, :] = values.astype(BF16).astype(F32)
+
+
+def finish_kernel(start, *refs):
+    finish_chunk(refs[:4], refs[4], refs[5], refs[6], start, refs[7], refs[8], 0)
+
+
+def finish(parts, cosine, sine, bias, start):
+    count = parts[0].shape[0] - STAT
+    return pl.pallas_call(
+        functools.partial(finish_kernel, start),
+        in_specs=[VMEM] * 7,
+        out_specs=[VMEM] * 2,
+        out_shape=[jax.ShapeDtypeStruct((count, HEAD_DIM), F32)] * 2,
+        compiler_params=params(24),
+        cost_estimate=cost(20 * count * 256, 2 * MIB),
+        name="finish",
+    )(*parts, cosine, sine, bias)
+
+
+def attend_kernel(starts, pages, page_rows, place_of, *refs):
+    parts, (cosine, sine, bias, near_queries, far_queries) = refs[:4], refs[4:9]
+    done = refs[9 : 9 + 2 * (len(starts) - 1)]
+    kept, sent, key_store, value_store = refs[9 + len(done) :]
+    for number, start in enumerate(starts[:-1]):
+        count = done[2 * number].shape[0]
+        key_store[start : start + count, :] = done[2 * number][...]
+        value_store[start : start + count, :] = done[2 * number + 1][...]
+    finish_chunk(parts, cosine, sine, bias, starts[-1], key_store, value_store, starts[-1])
+
+    core = place_of[0]
     lane_row = lax.broadcasted_iota(jnp.int32, (PAGE, HEAD_DIM), 1) // GROUPS
 
-    def attend(replica):
+    def attend(replica, query):
         key_pages, value_pages, masks = [], [], []
         for slot in range(SLOTS):
             page = pages[replica * SLOTS + slot]
@@ -238,7 +274,7 @@
             masks.append(lane_row == page_rows[replica * SLOTS + slot])
         keys = jnp.concatenate(key_pages, axis=0).astype(BF16)
         values = jnp.concatenate(value_pages, axis=0).astype(BF16)
-        scores = lax.dot_general(keys, queries[replica], NT, preferred_element_type=F32)
+        scores = lax.dot_general(keys, query, NT, preferred_element_type=F32)
         scores = scores * HEAD_DIM**-0.5
         scores = jnp.where(jnp.concatenate(masks, axis=0), scores, LOW)
         top = jnp.max(scores, axis=0, keepdims=True)
@@ -247,13 +283,13 @@
         summed = lax.dot_general(values, weights.astype(BF16), TN, preferred_element_type=F32)
         return summed.astype(BF16), split_stats(top, total)
 
-    for flip, out in ((1, sent), (0, kept)):
-
-        def block(step, carry, flip=flip, out=out):
+    for flip, queries, out in ((1, far_queries, sent), (0, near_queries, kept)):
+
+        def block(step, carry, flip=flip, queries=queries, out=out):
             for inner in range(4):
                 place = step * 4 + inner
-                replica = place * 2 + (core[0] + flip) % 2
-                summed, stats = attend(replica)
+                replica = place * 2 + (core + flip) % 2
+                summed, stats = attend(replica, queries[place])
                 out[place, 0:HEAD_DIM, :] = summed
                 out[place, HEAD_DIM : HEAD_DIM + STAT, :] = stats
             return carry
@@ -261,18 +297,18 @@
         lax.fori_loop(0, 4, block, 0)
 
 
-def finish(pages, page_rows, core, parts, cosine, sine, bias, queries):
+def attend(starts, pages, page_rows, place_of, parts, cosine, sine, bias, near, far, done):
     partial = jax.ShapeDtypeStruct((16, HEAD_DIM + STAT, HEAD_DIM), BF16)
     return pl.pallas_call(
-        finish_kernel,
-        in_specs=[SMEM] * 3 + [VMEM] * 12,
+        functools.partial(attend_kernel, starts),
+        in_specs=[SMEM] * 3 + [VMEM] * (9 + len(done)),
         out_specs=[VMEM, VMEM],
         out_shape=[partial, partial],
         scratch_shapes=[pltpu.VMEM((TOK, HEAD_DIM), F32)] * 2,
         compiler_params=params(32),
         cost_estimate=cost(4 * 2048 * 128 * 128, 16 * MIB),
-        name="finish",
-    )(pages, page_rows, core, *parts, cosine, sine, bias, queries)
+        name="attend",
+    )(pages, page_rows, place_of, *parts, cosine, sine, bias, near, far, *done)
 
 
 def merge_kernel(left, right, out):
@@ -374,43 +410,79 @@
     cache_values,
     lengths,
 ):
-    tp = lax.axis_index("tp")
-    core = lax.axis_index("rep") % 2
+    tp, rep = lax.axis_index("tp"), lax.axis_index("rep")
+    core = rep % 2
     x, y = tp // 2, tp % 2
-    query_heads = queries.reshape(ROWS * GROUPS, HEAD_DIM)
-    all_queries = lax.all_gather(query_heads, "rep", axis=0, tiled=False)
-    other = permute(prompt, lambda x, y, z, h, c: (x, y, z, h, 1 - c))
-
-    order = (2, 1, 3, 0)
-    weights = {}
-    for dx in order:
-        block = ((x + dx) % 4) * 2 + (y + core) % 2
-        rows = lax.dynamic_slice(kv_weight, (0, block * FEAT, 0), (2, FEAT, HEAD_DIM))
-        weights[dx] = permute(rows, lambda x, y, z, h, c, dx=dx: ((x + dx) % 4, y ^ c, z, h, y))
-
-    gain = lax.dynamic_slice(norm_gain, (tp * FEAT,), (FEAT,)).reshape(1, FEAT)
-    own_slot = ((y + core) % 2).reshape(1)
-    first, second, squares_first, squares_second = prepare(own_slot, prompt, other, gain)
-    tokens, squares = (first, second), (squares_first, squares_second)
+    starts = [sum(CHUNKS[:i]) for i in range(len(CHUNKS))]
+
+    def rows_of(number, follows=None):
+        start, count = starts[number], CHUNKS[number]
+        return after(prompt, follows)[start : start + count]
+
+    def swap(rows):
+        return permute(rows, lambda x, y, z, h, c: (x, 1 - y, z, h, c))
+
+    def weight_rows(block, follows=None):
+        return lax.dynamic_slice(
+            after(kv_weight, follows), (0, block * FEAT, 0), (2, FEAT, HEAD_DIM)
+        )
+
+    def fetch(dx, rows):
+        near = permute(rows, lambda x, y, z, h, c: ((x + dx) % 4, y, z, h, c))
+        return near, permute(near, lambda x, y, z, h, c: (x, y, z, h, 1 - c))
+
+    def wanted(dx, follows):
+        return weight_rows(((x + dx) % 4) * 2 + core, follows)
+
+    first_rows = rows_of(0)
+    others = [swap(first_rows)]
+    one = wanted(1, first_rows)
+    three = wanted(3, first_rows)
+    two = wanted(2, (one, three))
+    near, far = [None] * 4, [None] * 4
+    near[1], far[1] = fetch(1, one)
+    near[3], far[3] = fetch(3, three)
+    near[2], far[2] = fetch(2, two)
+    query_heads = after(queries, two).reshape(ROWS * GROUPS, HEAD_DIM)
+    groups = [[zy * 2 + c for zy in range(16)] for c in range(2)]
+    near_queries = lax.all_to_all(
+        jnp.broadcast_to(query_heads, (16, ROWS * GROUPS, HEAD_DIM)),
+        "rep", 0, 0, tiled=True, axis_index_groups=groups,
+    )
+    cosine, sine = angle_tables(page_offset)
+    others.append(swap(rows_of(1, (near[1], cosine, sine))))
+    near[0] = weight_rows(x * 2 + core, (far[1], far[3]))
+    far[0] = weight_rows(x * 2 + 1 - core, (far[1], far[3]))
+    far_queries = permute(
+        after(near_queries, near[2]), lambda x, y, z, h, c: (x, y, z, h, 1 - c)
+    )
+
+    def gain(block):
+        return lax.dynamic_slice(norm_gain, (block * FEAT,), (FEAT,)).reshape(1, FEAT)
+
+    own_gain, other_gain = gain(tp), gain(x * 2 + 1 - y)
+    same = (y == core).astype(jnp.int32).reshape(1)
+    bias = kv_bias.astype(F32)
 
     sums, tops, totals = resident(lengths, query_heads, cache_keys, cache_values)
-    cosine, sine = angle_tables(page_offset)
     pages, page_rows = page_tables(page_dest, page_row)
 
-    parts = []
-    for dx in order:
-        for k in range(2):
-            part = project(tokens[k], squares[k], weights[dx])
-            parts.append(
-                permute(part, lambda x, y, z, h, c, dx=dx, k=k: ((x - dx) % 4, c, z, h, y ^ k))
-            )
-
-    kept, sent = finish(
-        pages, page_rows, core.reshape(1), parts, cosine, sine, kv_bias.astype(F32), all_queries
+    done = []
+    for start, other in zip(starts, others):
+        outs = project(same, prompt, start, other, own_gain, other_gain, near, far)
+        parts = [outs[0]] + [
+            permute(outs[dx], lambda x, y, z, h, c, dx=dx: ((x - dx) % 4, y, z, h, c))
+            for dx in (1, 2, 3)
+        ]
+        if start != starts[-1]:
+            done.extend(finish(parts, cosine, sine, bias, start))
+
+    place_of = core.reshape(1)
+    kept, sent = attend(
+        starts, pages, page_rows, place_of, parts, cosine, sine, bias, near_queries, far_queries, done
     )
     arrived = permute(sent, lambda x, y, z, h, c: (x, y, z, h, 1 - c))
     merged = merge(kept, arrived)
-    groups = [[zy * 2 + c for zy in range(16)] for c in range(2)]
     received = lax.all_to_all(merged, "rep", 0, 0, tiled=True, axis_index_groups=groups)
     return conclude(received, sums, tops, totals)
 

time: 168 us -> 124 us (0.74)
  waiting for transfers between devices: 71.2 us -> 35.3 us
  between operations: 13.9 us -> 0.3 us
  starting transfers between devices: 26.7 us -> 38.9 us
  Pallas kernels: 40.1 us -> 31.5 us
    all_gather x1 -> x0, waiting for transfers between devices: 45.6 us -> none  [per_device(): all_queries = lax.all_gather(query_heads, 'rep', axis=0, tiled=False)]
    all_to_all x0 -> x1, starting transfers between devices: none -> 10.6 us  [per_device(): lax.all_to_all(jnp.broadcast_to(query_heads, (16, ROWS * GROUPS, HEAD_DIM...]
    ppermute x14 -> x16, waiting for transfers between devices: 12.7 us -> 22.6 us  [permute(): return lax.ppermute(array, ('rep', 'tp'), pairs)]
    pallas_call x10 -> x4, Pallas kernels: 31.6 us -> 23 us  [the longest x2 13.2 us: project(): pl.pallas_call(functools.partial(project_kernel, start), in_specs=[SMEM,...]
    all_to_all x1, starting transfers between devices: 4.41 us -> 10.5 us  [per_device(): lax.all_to_all(merged, 'rep', 0, 0, tiled=True, axis_index_groups=groups)]
    ppermute x14 -> x16, starting transfers between devices: 22.3 us -> 17.8 us  [permute(): return lax.ppermute(array, ('rep', 'tp'), pairs)]
    slice x0 -> x2, local copies, waits for them, and re-layouts: none -> 3.43 us  [rows_of(): return after(prompt, follows)[start:start + count]]
    unnamed x32 -> x28, local copies, waits for them, and re-layouts: 7.33 us -> 4.46 us
  transfers between devices with their start and end apart: 16 -> 18, of which waited for: 4 -> 9; matrix products, arithmetic and copies ran while one was open for 5% -> 8% of each run, Pallas kernels for 17% -> 17%
where the time goes in v2:
time: 124 us; the launch traced here: 123 us
  starting transfers between devices  38.9 us (31%)
  waiting for transfers between devices  35.3 us (28%)
  Pallas kernels  31.5 us (25%)
  local copies, waits for them, and re-layouts  14.1 us (11%)
  other arithmetic  2.65 us (2%)
    ppermute x16, waiting for transfers between devices, permute(): return lax.ppermute(array, ('rep', 'tp'), pairs)  22.6 us
    ppermute x16, starting transfers between devices, permute(): return lax.ppermute(array, ('rep', 'tp'), pairs)  17.8 us
    pallas_call x2, Pallas kernels, project(): pl.pallas_call(functools.partial(project_kernel, start), in_specs=[SMEM,...  13.2 us
    all_to_all x1, waiting for transfers between devices, per_device(): lax.all_to_all(merged, 'rep', 0, 0, tiled=True, axis_index_groups=groups)  12.7 us
    all_to_all x1, starting transfers between devices, per_device(): lax.all_to_all(jnp.broadcast_to(query_heads, (16, ROWS * GROUPS, HEAD_DIM...  10.6 us
    all_to_all x1, starting transfers between devices, per_device(): lax.all_to_all(merged, 'rep', 0, 0, tiled=True, axis_index_groups=groups)  10.5 us
    pallas_call x1, Pallas kernels, attend(): pl.pallas_call(functools.partial(attend_kernel, starts), in_specs=[SMEM]...  8.33 us
    pallas_call x1, Pallas kernels, resident(): pl.pallas_call(resident_kernel, grid=(ROWS,), in_specs=[SMEM, pl.BlockSpe...  6.48 us
  transfers between devices with their start and end apart: 18, of which 9 were waited for; matrix products, arithmetic and copies ran while one was open for 8% of the time, Pallas kernels for 17%

profile of v2, /device:TPU:8, one launch (start us, length us, event | category | flops | bytes accessed | tf_op | source)
XLA Modules:
  0.0 122.8 jit_solution(7377044126747270743)
XLA Ops:
  0.0 2.5 %slice.6 = bf16[640,1024]{1,0:T(8,128)(2,1)} slice(bf16[1024,1024]{1,0:T(8,128)(2,1)} %own.3), slice={[0:640], [0:1024]} | slice | bytes 2621440 | tf_op jit(solution)/shard_map/slice | solution.py:420
  2.5 2.2 %collective-permute-start.11 = (bf16[640,1024]{1,0:T(8,128)(2,1)}, bf16[640,1024]{1,0:T(8,128)(2,1)}, u32[]{:S(2)}, u32[]{:S(2)}) collective-permute-start(bf16[640,1024]{1,0:T(8,128)(2,1)} %slice.6), channel_id=1, source_target_pairs={{0,1},{8,9},{16,17},{24,25},{32,33},{40,41},{48,49},{56,57},{64,65... | collective-permute-start | bytes 3932168 | tf_op jit(solution)/shard_map/ppermute | solution.py:56
  4.7 2.1 %constant_dynamic-slice_fusion.3 = (bf16[2,1024,128]{2,1,0:T(8,128)(2,1)S(1)}, bf16[2,1024,128]{2,1,0:T(8,128)(2,1)}) fusion(bf16[2,8192,128]{2,1,0:T(8,128)(2,1)} %param.13, s32[]{:T(128)S(6)} %select_n.65, s32[]{:T(128)S(6)} %select_n.61), kind=kLoop, calls=%fused_computation.15 | loop fusion | bytes 2097160 | tf_op jit(solution)/shard_map/dynamic_slice | solution.py:426
  6.7 1.1 constant_dynamic-slice_fusion.1
  7.8 1.4 %collective-permute-start.5 = (bf16[2,1024,128]{2,1,0:T(8,128)(2,1)S(1)}, bf16[2,1024,128]{2,1,0:T(8,128)(2,1)}, u32[]{:S(2)}, u32[]{:S(2)}) collective-permute-start(bf16[2,1024,128]{2,1,0:T(8,128)(2,1)S(1)} %constant_dynamic-slice_fusion.1), channel_id=1, source_target_pairs={{0,4},{8,12},{16,20},{24,28},{32,36},{40,44},{48,52},{56,60},{64,6... | collective-permute-start | bytes 1572872 | tf_op jit(solution)/shard_map/ppermute | solution.py:56
  9.2 0.6 collective-permute-start
  9.8 2.6 %collective-permute-start.3 = (bf16[2,1024,128]{2,1,0:T(8,128)(2,1)S(1)}, bf16[2,1024,128]{2,1,0:T(8,128)(2,1)}, u32[]{:S(2)}, u32[]{:S(2)}) collective-permute-start(bf16[2,1024,128]{2,1,0:T(8,128)(2,1)S(1)} %get-tuple-element.51), channel_id=1, source_target_pairs={{0,6},{8,14},{16,22},{24,30},{32,38},{40,46},{48,54},{56,62},{64,7... | collective-permute-start | bytes 1572872 | tf_op jit(solution)/shard_map/ppermute | solution.py:56
  12.5 1.0 broadcast_in_dim.39
  13.4 10.6 %all-to-all-start = ((bf16[16,128,128]{2,1,0:T(8,128)(2,1)}), bf16[16,128,128]{2,1,0:T(8,128)(2,1)}, u32[]{:S(2)}, u32[]{:S(2)}) async-start(bf16[16,128,128]{2,1,0:T(8,128)(2,1)} %broadcast_in_dim.39), calls=%async_computation | async-start | bytes 1048576 | tf_op jit(solution)/shard_map/all_to_all | solution.py:448
  24.1 0.1 add_convert_fusion
  24.2 0.1 convert_element_type.19
  24.3 0.1 collective-permute-done.5.refs_2_
  24.4 7.8 %collective-permute-done.refs_1_ = bf16[2,1024,128]{2,1,0:T(8,128)(2,1)} collective-permute-done((bf16[2,1024,128]{2,1,0:T(8,128)(2,1)}, bf16[2,1024,128]{2,1,0:T(8,128)(2,1)}, u32[]{:S(2)}, u32[]{:S(2)}) %collective-permute-start) | collective-permute-done | bytes 524320 | tf_op jit(solution)/shard_map/ppermute | solution.py:56
  32.3 0.3 collective-permute-done.3.refs_3_
  32.5 0.2 collective-permute-start.4
  32.8 1.9 %fusion = (f32[1024,64]{1,0:T(8,128)S(1)}, f32[1024,64]{1,0:T(8,128)S(1)}, f32[1024,64]{1,0:T(8,128)S(1)}) fusion(f32[64]{0:T(128)S(1)} %multiply_exponential_fusion, f32[1024]{0:T(1024)S(1)} %convert_element_type.19), kind=kLoop, calls=%fused_computation.4 | loop fusion | flops 131072 | bytes 790784 | tf_op jit(solution)/shard_map/neg | solution.py:385
  34.7 0.3 pad_maximum_fusion
  35.0 0.9 slice.7
  36.0 1.7 %collective-permute-start.1 = (bf16[384,1024]{1,0:T(8,128)(2,1)}, bf16[384,1024]{1,0:T(8,128)(2,1)}, u32[]{:S(2)}, u32[]{:S(2)}) collective-permute-start(bf16[384,1024]{1,0:T(8,128)(2,1)} %slice.7), channel_id=1, source_target_pairs={{0,1},{8,9},{16,17},{24,25},{32,33},{40,41},{48,49},{56,57},{64,65... | collective-permute-start | bytes 2359304 | tf_op jit(solution)/shard_map/ppermute | solution.py:56
  37.7 0.7 fusion.2
  38.4 1.3 %constant_dynamic-slice_fusion = (bf16[2,1024,128]{2,1,0:T(8,128)(2,1)S(1)}, bf16[2,1024,128]{2,1,0:T(8,128)(2,1)S(1)}) fusion(bf16[2,8192,128]{2,1,0:T(8,128)(2,1)} %param.13, s32[]{:T(128)S(6)} %select_n.69, s32[]{:T(128)S(6)} %select_n.66), kind=kLoop, calls=%fused_computation.12 | loop fusion | bytes 2097160 | tf_op jit(solution)/shard_map/dynamic_slice | solution.py:426
  39.7 7.2 %project.3 = (bf16[656,256]{1,0:T(8,128)(2,1)S(1)}, bf16[656,256]{1,0:T(8,128)(2,1)}, bf16[656,256]{1,0:T(8,128)(2,1)}, bf16[656,256]{1,0:T(8,128)(2,1)S(1)}) custom-call(s32[1]{0:T(128)} %bitcast.2.same, bf16[1024,1024]{1,0:T(8,128)(2,1)S(1)} %copy-done, bf16[640,1024]{1,0:T(8,128)(2,1)} %collective-permute-done.11.other, f32[1,1024]{1,0:T(1,128)S(1)} %bitcast.8, ...), custom_call_target="tpu_custom_call" | custom-call | flops 2684354560 | bytes 6291456 | tf_op jit(solution)/shard_map/project/pallas_call | solution.py:132
  46.9 0.7 copy-done.8
  47.7 2.3 %collective-permute-start.12 = (bf16[656,256]{1,0:T(8,128)(2,1)}, bf16[656,256]{1,0:T(8,128)(2,1)}, u32[]{:S(2)}, u32[]{:S(2)}) collective-permute-start(bf16[656,256]{1,0:T(8,128)(2,1)} %get-tuple-element.37), channel_id=1, source_target_pairs={{0,6},{8,14},{16,22},{24,30},{32,38},{40,46},{48,54},{56,62},{64,7... | collective-permute-start | bytes 1007624 | tf_op jit(solution)/shard_map/ppermute | solution.py:56
  49.9 1.4 %collective-permute-start.13 = (bf16[656,256]{1,0:T(8,128)(2,1)}, bf16[656,256]{1,0:T(8,128)(2,1)}, u32[]{:S(2)}, u32[]{:S(2)}) collective-permute-start(bf16[656,256]{1,0:T(8,128)(2,1)} %get-tuple-element.38), channel_id=1, source_target_pairs={{0,4},{8,12},{16,20},{24,28},{32,36},{40,44},{48,52},{56,60},{64,6... | collective-permute-start | bytes 1007624 | tf_op jit(solution)/shard_map/ppermute | solution.py:56
  51.3 0.2 convert_reduce_fusion
  51.5 0.2 collective-permute-start.14
  51.8 4.6 %collective-permute-done.1.other = bf16[384,1024]{1,0:T(8,128)(2,1)} collective-permute-done((bf16[384,1024]{1,0:T(8,128)(2,1)}, bf16[384,1024]{1,0:T(8,128)(2,1)}, u32[]{:S(2)}, u32[]{:S(2)}) %collective-permute-start.1) | collective-permute-done | bytes 786464 | tf_op jit(solution)/shard_map/ppermute | solution.py:56
  56.4 1.0 copy-done.4
  57.4 1.0 copy-done.6
  58.4 6.0 %project.2 = (bf16[400,256]{1,0:T(8,128)(2,1)S(1)}, bf16[400,256]{1,0:T(8,128)(2,1)S(1)}, bf16[400,256]{1,0:T(8,128)(2,1)S(1)}, bf16[400,256]{1,0:T(8,128)(2,1)S(1)}) custom-call(s32[1]{0:T(128)} %bitcast.2.same, bf16[1024,1024]{1,0:T(8,128)(2,1)S(1)} %copy-done, bf16[384,1024]{1,0:T(8,128)(2,1)} %collective-permute-done.1.other, f32[1,1024]{1,0:T(1,128)S(1)} %bitcast.9, ...), custom_call_target="tpu_custom_call" | custom-call | flops 1610612736 | bytes 6291456 | tf_op jit(solution)/shard_map/project/pallas_call | solution.py:132
  64.5 2.4 %collective-permute-start.7 = (bf16[400,256]{1,0:T(8,128)(2,1)S(1)}, bf16[400,256]{1,0:T(8,128)(2,1)S(1)}, u32[]{:S(2)}, u32[]{:S(2)}) collective-permute-start(bf16[400,256]{1,0:T(8,128)(2,1)S(1)} %get-tuple-element.31), channel_id=1, source_target_pairs={{0,6},{8,14},{16,22},{24,30},{32,38},{40,46},{48,54},{56,62},{64,7... | collective-permute-start | bytes 614408 | tf_op jit(solution)/shard_map/ppermute | solution.py:56
  66.8 0.9 collective-permute-start.8
  67.7 1.8 %collective-permute-start.9 = (bf16[400,256]{1,0:T(8,128)(2,1)S(1)}, bf16[400,256]{1,0:T(8,128)(2,1)S(1)}, u32[]{:S(2)}, u32[]{:S(2)}) collective-permute-start(bf16[400,256]{1,0:T(8,128)(2,1)S(1)} %get-tuple-element.33), channel_id=1, source_target_pairs={{0,2},{8,10},{16,18},{24,26},{32,34},{40,42},{48,50},{56,58},{64,6... | collective-permute-start | bytes 614408 | tf_op jit(solution)/shard_map/ppermute | solution.py:56
  69.6 0.1 select_reduce_fusion
  69.7 1.5 %finish.1 = (f32[640,128]{1,0:T(8,128)S(1)}, f32[640,128]{1,0:T(8,128)S(1)}) custom-call(bf16[656,256]{1,0:T(8,128)(2,1)S(1)} %get-tuple-element.36.refs_0_, bf16[656,256]{1,0:T(8,128)(2,1)} %collective-permute-done.12.refs_1_, bf16[656,256]{1,0:T(8,128)(2,1)} %collective-permute-done.13.refs_2_, bf16[656,256]{1,0:T(8,128)(2,1)S(1)} %collective-permute-done.14.refs_3_, ...), custom_call_target="tpu_custom_call" | custom-call | flops 3276800 | bytes 2097152 | tf_op jit(solution)/shard_map/finish/pallas_call | solution.py:243
  71.3 4.2 %collective-permute-done.7.refs_1_ = bf16[400,256]{1,0:T(8,128)(2,1)S(1)} collective-permute-done((bf16[400,256]{1,0:T(8,128)(2,1)S(1)}, bf16[400,256]{1,0:T(8,128)(2,1)S(1)}, u32[]{:S(2)}, u32[]{:S(2)}) %collective-permute-start.7) | collective-permute-done | bytes 204832 | tf_op jit(solution)/shard_map/ppermute | solution.py:56
  75.5 0.9 collective-permute-done.8.refs_2_
  76.3 2.7 %collective-permute-done.9.refs_3_ = bf16[400,256]{1,0:T(8,128)(2,1)S(1)} collective-permute-done((bf16[400,256]{1,0:T(8,128)(2,1)S(1)}, bf16[400,256]{1,0:T(8,128)(2,1)S(1)}, u32[]{:S(2)}, u32[]{:S(2)}) %collective-permute-start.9) | collective-permute-done | bytes 204832 | tf_op jit(solution)/shard_map/ppermute | solution.py:56
  79.0 8.3 %attend.1 = (bf16[16,144,128]{2,1,0:T(8,128)(2,1)S(1)}, bf16[16,144,128]{2,1,0:T(8,128)(2,1)S(1)}) custom-call(s32[256]{0:T(256)S(1)} %get-tuple-element.48.pages, s32[256]{0:T(256)S(1)} %get-tuple-element.47.page_rows, s32[1]{0:T(128)} %bitcast.1.place_of, bf16[400,256]{1,0:T(8,128)(2,1)S(1)} %get-tuple-element.30.refs_0_, ...), custom_call_target="tpu_custom_call" | custom-call | flops 134217728 | bytes 16777216 | tf_op jit(solution)/shard_map/attend/pallas_call | solution.py:302
  87.4 0.1 collective-permute-start.15
  87.5 2.0 %collective-permute-done.15.right = bf16[16,144,128]{2,1,0:T(8,128)(2,1)S(1)} collective-permute-done((bf16[16,144,128]{2,1,0:T(8,128)(2,1)S(1)}, bf16[16,144,128]{2,1,0:T(8,128)(2,1)S(1)}, u32[]{:S(2)}, u32[]{:S(2)}) %collective-permute-start.15) | collective-permute-done | bytes 589856 | tf_op jit(solution)/shard_map/ppermute | solution.py:56
  89.5 1.2 merge.1
  90.7 10.5 %all-to-all-start.1 = ((bf16[16,144,128]{2,1,0:T(8,128)(2,1)}), bf16[16,144,128]{2,1,0:T(8,128)(2,1)S(1)}, u32[]{:S(2)}, u32[]{:S(2)}) async-start(bf16[16,144,128]{2,1,0:T(8,128)(2,1)} %merge.1), calls=%async_computation.1 | async-start | bytes 1179648 | tf_op jit(solution)/shard_map/all_to_all | solution.py:486
  101.2 1.6 %copy-done.2 = bf16[16,512,128]{2,1,0:T(8,128)(2,1)S(1)} copy-done((bf16[16,512,128]{2,1,0:T(8,128)(2,1)S(1)}, bf16[16,512,128]{2,1,0:T(8,128)(2,1)}, u32[]{:S(2)}) %copy-start.2) | copy-done | bytes 2097176
  102.8 6.5 %resident.1 = (f32[128,128]{1,0:T(8,128)S(1)}, f32[8,128]{1,0:T(8,128)S(1)}, f32[8,128]{1,0:T(8,128)S(1)}) custom-call(s32[16]{0:T(128)S(1)} %copy-done.7, bf16[128,128]{1,0:T(8,128)(2,1)S(1)} %reshape.52.queries, bf16[16,512,128]{2,1,0:T(8,128)(2,1)S(1)} %copy-done.1, bf16[16,512,128]{2,1,0:T(8,128)(2,1)S(1)} %copy-done.2), custom_call_target="tpu_custom_call" | custom-call | flops 33554432 | bytes 16777216 | tf_op jit(solution)/shard_map/resident/pallas_call | solution.py:177
  109.3 12.7 %all-to-all-done.1.received = bf16[16,144,128]{2,1,0:T(8,128)(2,1)S(1)} async-done(((bf16[16,144,128]{2,1,0:T(8,128)(2,1)}), bf16[16,144,128]{2,1,0:T(8,128)(2,1)S(1)}, u32[]{:S(2)}, u32[]{:S(2)}) %all-to-all-start.1) | async-done | bytes 589856 | tf_op jit(solution)/shard_map/all_to_all | solution.py:486
  121.9 0.9 conclude.1
  (40 shorter events, 0.1 us)
Async XLA Ops:
  2.5 10.0 %copy-start.9 = (bf16[16,1024]{1,0:T(8,128)(2,1)S(1)}, bf16[16,1024]{1,0:T(8,128)(2,1)}, u32[]{:S(2)}) copy-start(bf16[16,1024]{1,0:T(8,128)(2,1)} %param.18) | copy-start | bytes 98308
  2.5 37.2 %collective-permute-start.11 = (bf16[640,1024]{1,0:T(8,128)(2,1)}, bf16[640,1024]{1,0:T(8,128)(2,1)}, u32[]{:S(2)}, u32[]{:S(2)}) collective-permute-start(bf16[640,1024]{1,0:T(8,128)(2,1)} %slice.6), channel_id=1, source_target_pairs={{0,1},{8,9},{16,17},{24,25},{32,33},{40,41},{48,49},{56,57},{64,65... | collective-permute-start | bytes 3932168 | tf_op jit(solution)/shard_map/ppermute | solution.py:56
  4.7 19.4 %copy-start.10 = (s32[128]{0:T(128)S(1)}, s32[128]{0:T(128)}, u32[]{:S(2)}) copy-start(s32[128]{0:T(128)} %param.17) | copy-start | bytes 1540
  7.8 16.6 %collective-permute-start.5 = (bf16[2,1024,128]{2,1,0:T(8,128)(2,1)S(1)}, bf16[2,1024,128]{2,1,0:T(8,128)(2,1)}, u32[]{:S(2)}, u32[]{:S(2)}) collective-permute-start(bf16[2,1024,128]{2,1,0:T(8,128)(2,1)S(1)} %constant_dynamic-slice_fusion.1), channel_id=1, source_target_pairs={{0,4},{8,12},{16,20},{24,28},{32,36},{40,44},{48,52},{56,60},{64,6... | collective-permute-start | bytes 1572872 | tf_op jit(solution)/shard_map/ppermute | solution.py:56
  9.2 23.0 %collective-permute-start = (bf16[2,1024,128]{2,1,0:T(8,128)(2,1)}, bf16[2,1024,128]{2,1,0:T(8,128)(2,1)}, u32[]{:S(2)}, u32[]{:S(2)}) collective-permute-start(bf16[2,1024,128]{2,1,0:T(8,128)(2,1)} %get-tuple-element.52), channel_id=1, source_target_pairs={{0,2},{8,10},{16,18},{24,26},{32,34},{40,42},{48,50},{56,58},{64,6... | collective-permute-start | bytes 1572872 | tf_op jit(solution)/shard_map/ppermute | solution.py:56
  9.8 22.7 %collective-permute-start.3 = (bf16[2,1024,128]{2,1,0:T(8,128)(2,1)S(1)}, bf16[2,1024,128]{2,1,0:T(8,128)(2,1)}, u32[]{:S(2)}, u32[]{:S(2)}) collective-permute-start(bf16[2,1024,128]{2,1,0:T(8,128)(2,1)S(1)} %get-tuple-element.51), channel_id=1, source_target_pairs={{0,6},{8,14},{16,22},{24,30},{32,38},{40,46},{48,54},{56,62},{64,7... | collective-permute-start | bytes 1572872 | tf_op jit(solution)/shard_map/ppermute | solution.py:56
  13.4 37.9 %all-to-all-start = ((bf16[16,128,128]{2,1,0:T(8,128)(2,1)}), bf16[16,128,128]{2,1,0:T(8,128)(2,1)}, u32[]{:S(2)}, u32[]{:S(2)}) async-start(bf16[16,128,128]{2,1,0:T(8,128)(2,1)} %broadcast_in_dim.39), calls=%async_computation | async-start | bytes 1048576 | tf_op jit(solution)/shard_map/all_to_all | solution.py:448
  24.3 10.7 %copy-start = (bf16[1024,1024]{1,0:T(8,128)(2,1)S(1)}, bf16[1024,1024]{1,0:T(8,128)(2,1)}, u32[]{:S(2)}) copy-start(bf16[1024,1024]{1,0:T(8,128)(2,1)} %own.3) | copy-start | bytes 6291460
  24.4 15.3 %collective-permute-start.6 = (bf16[2,1024,128]{2,1,0:T(8,128)(2,1)}, bf16[2,1024,128]{2,1,0:T(8,128)(2,1)}, u32[]{:S(2)}, u32[]{:S(2)}) collective-permute-start(bf16[2,1024,128]{2,1,0:T(8,128)(2,1)} %collective-permute-done.5.refs_2_), channel_id=1, source_target_pairs={{0,8},{8,0},{16,24},{24,16},{32,40},{40,32},{48,56},{56,48},{64,72... | collective-permute-start | bytes 1572872 | tf_op jit(solution)/shard_map/ppermute | solution.py:56
  32.2 6.2 %collective-permute-start.2 = (bf16[2,1024,128]{2,1,0:T(8,128)(2,1)}, bf16[2,1024,128]{2,1,0:T(8,128)(2,1)}, u32[]{:S(2)}, u32[]{:S(2)}) collective-permute-start(bf16[2,1024,128]{2,1,0:T(8,128)(2,1)} %collective-permute-done.refs_1_), channel_id=1, source_target_pairs={{0,8},{8,0},{16,24},{24,16},{32,40},{40,32},{48,56},{56,48},{64,72... | collective-permute-start | bytes 1572872 | tf_op jit(solution)/shard_map/ppermute | solution.py:56
  32.5 5.9 %collective-permute-start.4 = (bf16[2,1024,128]{2,1,0:T(8,128)(2,1)}, bf16[2,1024,128]{2,1,0:T(8,128)(2,1)}, u32[]{:S(2)}, u32[]{:S(2)}) collective-permute-start(bf16[2,1024,128]{2,1,0:T(8,128)(2,1)} %collective-permute-done.3.refs_3_), channel_id=1, source_target_pairs={{0,8},{8,0},{16,24},{24,16},{32,40},{40,32},{48,56},{56,48},{64,72... | collective-permute-start | bytes 1572872 | tf_op jit(solution)/shard_map/ppermute | solution.py:56
  36.0 20.4 %collective-permute-start.1 = (bf16[384,1024]{1,0:T(8,128)(2,1)}, bf16[384,1024]{1,0:T(8,128)(2,1)}, u32[]{:S(2)}, u32[]{:S(2)}) collective-permute-start(bf16[384,1024]{1,0:T(8,128)(2,1)} %slice.7), channel_id=1, source_target_pairs={{0,1},{8,9},{16,17},{24,25},{32,33},{40,41},{48,49},{56,57},{64,65... | collective-permute-start | bytes 2359304 | tf_op jit(solution)/shard_map/ppermute | solution.py:56
  39.7 7.2 %copy-start.3 = (bf16[2,1024,128]{2,1,0:T(8,128)(2,1)}, bf16[2,1024,128]{2,1,0:T(8,128)(2,1)S(1)}, u32[]{:S(2)}) copy-start(bf16[2,1024,128]{2,1,0:T(8,128)(2,1)S(1)} %get-tuple-element.49.refs_4_) | copy-start | bytes 1572868
  39.7 7.2 %copy-start.5 = (bf16[2,1024,128]{2,1,0:T(8,128)(2,1)}, bf16[2,1024,128]{2,1,0:T(8,128)(2,1)S(1)}, u32[]{:S(2)}) copy-start(bf16[2,1024,128]{2,1,0:T(8,128)(2,1)S(1)} %get-tuple-element.50.refs_0_) | copy-start | bytes 1572868
  39.7 11.6 %copy-start.12 = (s32[128,1]{0,1:T(1,128)S(1)}, s32[128,1]{0,1:T(1,128)}, u32[]{:S(2)}) copy-start(s32[128,1]{0,1:T(1,128)} %param.15) | copy-start | bytes 1540
  46.9 0.7 copy-start.8
  47.7 19.1 %collective-permute-start.12 = (bf16[656,256]{1,0:T(8,128)(2,1)}, bf16[656,256]{1,0:T(8,128)(2,1)}, u32[]{:S(2)}, u32[]{:S(2)}) collective-permute-start(bf16[656,256]{1,0:T(8,128)(2,1)} %get-tuple-element.37), channel_id=1, source_target_pairs={{0,6},{8,14},{16,22},{24,30},{32,38},{40,46},{48,54},{56,62},{64,7... | collective-permute-start | bytes 1007624 | tf_op jit(solution)/shard_map/ppermute | solution.py:56
  49.9 17.8 %collective-permute-start.13 = (bf16[656,256]{1,0:T(8,128)(2,1)}, bf16[656,256]{1,0:T(8,128)(2,1)}, u32[]{:S(2)}, u32[]{:S(2)}) collective-permute-start(bf16[656,256]{1,0:T(8,128)(2,1)} %get-tuple-element.38), channel_id=1, source_target_pairs={{0,4},{8,12},{16,20},{24,28},{32,36},{40,44},{48,52},{56,60},{64,6... | collective-permute-start | bytes 1007624 | tf_op jit(solution)/shard_map/ppermute | solution.py:56
  51.3 19.9 %collective-permute-start.10 = (bf16[16,128,128]{2,1,0:T(8,128)(2,1)}, bf16[16,128,128]{2,1,0:T(8,128)(2,1)S(1)}, u32[]{:S(2)}, u32[]{:S(2)}) collective-permute-start(bf16[16,128,128]{2,1,0:T(8,128)(2,1)} %all-to-all-done.refs_7_), channel_id=1, source_target_pairs={{0,8},{8,0},{16,24},{24,16},{32,40},{40,32},{48,56},{56,48},{64,72... | collective-permute-start | bytes 1572872 | tf_op jit(solution)/shard_map/ppermute | solution.py:56
  51.5 18.0 %copy-start.13 = (bf16[2,128]{1,0:T(2,128)(2,1)S(1)}, bf16[2,128]{1,0:T(2,128)(2,1)}, u32[]{:S(2)}) copy-start(bf16[2,128]{1,0:T(2,128)(2,1)} %param.14) | copy-start | bytes 1540
  51.5 18.0 %copy-start.11 = (s32[128]{0:T(128)S(1)}, s32[128]{0:T(128)}, u32[]{:S(2)}) copy-start(s32[128]{0:T(128)} %param.16) | copy-start | bytes 1540
  51.5 18.2 %collective-permute-start.14 = (bf16[656,256]{1,0:T(8,128)(2,1)}, bf16[656,256]{1,0:T(8,128)(2,1)S(1)}, u32[]{:S(2)}, u32[]{:S(2)}) collective-permute-start(bf16[656,256]{1,0:T(8,128)(2,1)} %copy-done.8), channel_id=1, source_target_pairs={{0,2},{8,10},{16,18},{24,26},{32,34},{40,42},{48,50},{56,58},{64,6... | collective-permute-start | bytes 1007624 | tf_op jit(solution)/shard_map/ppermute | solution.py:56
  56.4 1.0 copy-start.4
  57.4 1.0 copy-start.6
  64.5 11.0 %collective-permute-start.7 = (bf16[400,256]{1,0:T(8,128)(2,1)S(1)}, bf16[400,256]{1,0:T(8,128)(2,1)S(1)}, u32[]{:S(2)}, u32[]{:S(2)}) collective-permute-start(bf16[400,256]{1,0:T(8,128)(2,1)S(1)} %get-tuple-element.31), channel_id=1, source_target_pairs={{0,6},{8,14},{16,22},{24,30},{32,38},{40,46},{48,54},{56,62},{64,7... | collective-permute-start | bytes 614408 | tf_op jit(solution)/shard_map/ppermute | solution.py:56
  66.8 9.5 %collective-permute-start.8 = (bf16[400,256]{1,0:T(8,128)(2,1)S(1)}, bf16[400,256]{1,0:T(8,128)(2,1)S(1)}, u32[]{:S(2)}, u32[]{:S(2)}) collective-permute-start(bf16[400,256]{1,0:T(8,128)(2,1)S(1)} %get-tuple-element.32), channel_id=1, source_target_pairs={{0,4},{8,12},{16,20},{24,28},{32,36},{40,44},{48,52},{56,60},{64,6... | collective-permute-start | bytes 614408 | tf_op jit(solution)/shard_map/ppermute | solution.py:56
  67.7 11.3 %collective-permute-start.9 = (bf16[400,256]{1,0:T(8,128)(2,1)S(1)}, bf16[400,256]{1,0:T(8,128)(2,1)S(1)}, u32[]{:S(2)}, u32[]{:S(2)}) collective-permute-start(bf16[400,256]{1,0:T(8,128)(2,1)S(1)} %get-tuple-element.33), channel_id=1, source_target_pairs={{0,2},{8,10},{16,18},{24,26},{32,34},{40,42},{48,50},{56,58},{64,6... | collective-permute-start | bytes 614408 | tf_op jit(solution)/shard_map/ppermute | solution.py:56
  87.4 13.8 %copy-start.1 = (bf16[16,512,128]{2,1,0:T(8,128)(2,1)S(1)}, bf16[16,512,128]{2,1,0:T(8,128)(2,1)}, u32[]{:S(2)}) copy-start(bf16[16,512,128]{2,1,0:T(8,128)(2,1)} %keys.1) | copy-start | bytes 6291460
  87.4 13.8 %copy-start.7 = (s32[16]{0:T(128)S(1)}, s32[16]{0:T(128)}, u32[]{:S(2)}) copy-start(s32[16]{0:T(128)} %lengths.1) | copy-start | bytes 196
  87.4 2.1 %collective-permute-start.15 = (bf16[16,144,128]{2,1,0:T(8,128)(2,1)S(1)}, bf16[16,144,128]{2,1,0:T(8,128)(2,1)S(1)}, u32[]{:S(2)}, u32[]{:S(2)}) collective-permute-start(bf16[16,144,128]{2,1,0:T(8,128)(2,1)S(1)} %get-tuple-element.43), channel_id=1, source_target_pairs={{0,8},{8,0},{16,24},{24,16},{32,40},{40,32},{48,56},{56,48},{64,72... | collective-permute-start | bytes 1769480 | tf_op jit(solution)/shard_map/ppermute | solution.py:56
  90.7 31.3 %all-to-all-start.1 = ((bf16[16,144,128]{2,1,0:T(8,128)(2,1)}), bf16[16,144,128]{2,1,0:T(8,128)(2,1)S(1)}, u32[]{:S(2)}, u32[]{:S(2)}) async-start(bf16[16,144,128]{2,1,0:T(8,128)(2,1)} %merge.1), calls=%async_computation.1 | async-start | bytes 1179648 | tf_op jit(solution)/shard_map/all_to_all | solution.py:486
  101.2 1.6 %copy-start.2 = (bf16[16,512,128]{2,1,0:T(8,128)(2,1)S(1)}, bf16[16,512,128]{2,1,0:T(8,128)(2,1)}, u32[]{:S(2)}) copy-start(bf16[16,512,128]{2,1,0:T(8,128)(2,1)} %values.1) | copy-start | bytes 6291460

commit v3 on v2

--- a/solution.py
+++ b/solution.py
@@ -18,7 +18,7 @@
 GROUPS = 8
 CONTEXT = 512
 TILE = 128
-CHUNKS = (640, 384)
+CHUNKS = (512, 512)
 STEP = 32
 STAT = 16
 LOW = -1e30
@@ -62,45 +62,43 @@
     return lax.optimization_barrier((value, other))[0]
 
 
-def project_kernel(start, same, own, other, own_gain, other_gain, *refs):
+def project_kernel(start, same, own, other, *refs):
     weights, outs = refs[0:8], refs[8:12]
-    tokens_store, scaled, folded, store, results, arrived, left = refs[12:]
+    tokens, folded, store, results, arrived, left = refs[12:]
     count = other.shape[0]
+    own_place = 1 - same[0]
     copies = [
-        pltpu.make_async_copy(own.at[pl.ds(start, count), :], tokens_store.at[0], arrived.at[8]),
-        pltpu.make_async_copy(other, tokens_store.at[1], arrived.at[9]),
+        pltpu.make_async_copy(own.at[pl.ds(start, count), :], tokens.at[own_place], arrived.at[8]),
+        pltpu.make_async_copy(other, tokens.at[1 - own_place], arrived.at[9]),
     ]
-    for head in (2, 1, 3, 0):
+    heads = (2, 1, 3, 0)
+    for head in heads:
         for i in (head, head + 4):
             copies.append(pltpu.make_async_copy(weights[i], store.at[i], arrived.at[i]))
-    for copy in copies[:4]:
+    for copy in copies:
         copy.start()
-    ones = jnp.ones((8, TILE), BF16)
-
     copies[0].wait()
     copies[1].wait()
-    for copy in copies[4:]:
-        copy.start()
-
-    def scale(step, carry):
+
+    def square(step, carry):
         rows = pl.ds(pl.multiple_of(step * STEP, STEP), STEP)
-        own_values, other_values = (tokens_store[i, rows, :].astype(F32) for i in (0, 1))
-        square = own_values * own_values + other_values * other_values
-        sums = square[:, 0:TILE]
+        left_values, right_values = (tokens[i, rows, :].astype(F32) for i in (0, 1))
+        squares = left_values * left_values + right_values * right_values
+        sums = squares[:, 0:TILE]
         for part in range(1, FEAT // TILE):
-            sums = sums + square[:, part * TILE : (part + 1) * TILE]
+            sums = sums + squares[:, part * TILE : (part + 1) * TILE]
         folded[rows, :] = sums
-        scaled[1 - same[0], rows, :] = (own_values * own_gain[...]).astype(BF16)
-        scaled[same[0], rows, :] = (other_values * other_gain[...]).astype(BF16)
         return carry
 
-    lax.fori_loop(0, count // STEP, scale, 0)
+    lax.fori_loop(0, count // STEP, square, 0)
+    ones = jnp.ones((8, TILE), BF16)
     high = folded[...].astype(BF16)
     low = (folded[...] - high.astype(F32)).astype(BF16)
     total = lax.dot_general(ones, high, NT, preferred_element_type=F32)
     total = (total + lax.dot_general(ones, low, NT, preferred_element_type=F32))[0:1, :]
     top = total.astype(BF16).astype(F32)
     rest = total - top
+
     index = lax.broadcasted_iota(jnp.int32, (STAT, TILE), 0)
     table = jnp.zeros((STAT, TILE), F32)
     for tile in range(count // TILE):
@@ -110,15 +108,15 @@
     table = jnp.concatenate([table, jnp.zeros_like(table)], axis=1).astype(BF16)
 
     leaving = []
-    for number, head in enumerate((2, 1, 3, 0)):
+    for number, head in enumerate(heads):
         copies[2 + 2 * number].wait()
         copies[3 + 2 * number].wait()
         near = jnp.concatenate([store[head, 0], store[head, 1]], axis=1)
         far = jnp.concatenate([store[head + 4, 0], store[head + 4, 1]], axis=1)
         for tile in range(0, count, TILE):
             rows = slice(tile, tile + TILE)
-            part = jnp.dot(scaled[0, rows, :], near, preferred_element_type=F32)
-            part = part + jnp.dot(scaled[1, rows, :], far, preferred_element_type=F32)
+            part = jnp.dot(tokens[0, rows, :], near, preferred_element_type=F32)
+            part = part + jnp.dot(tokens[1, rows, :], far, preferred_element_type=F32)
             results[head, rows, :] = part.astype(BF16)
         results[head, count:, :] = table
         leaving.append(pltpu.make_async_copy(results.at[head], outs[head], left.at[head]))
@@ -127,15 +125,14 @@
         copy.wait()
 
 
-def project(same, prompt, start, other, own_gain, other_gain, near, far):
+def project(same, prompt, start, other, near, far):
     count = other.shape[0]
     return pl.pallas_call(
         functools.partial(project_kernel, start),
-        in_specs=[SMEM, HBM, HBM, VMEM, VMEM] + [HBM] * 8,
+        in_specs=[SMEM] + [HBM] * 10,
         out_specs=[HBM] * 4,
         out_shape=[jax.ShapeDtypeStruct((count + STAT, 2 * HEAD_DIM), BF16)] * 4,
         scratch_shapes=[
-            pltpu.VMEM((2, count, FEAT), BF16),
             pltpu.VMEM((2, count, FEAT), BF16),
             pltpu.VMEM((count, TILE), F32),
             pltpu.VMEM((8, 2, FEAT, HEAD_DIM), BF16),
@@ -143,10 +140,10 @@
             pltpu.SemaphoreType.DMA((10,)),
             pltpu.SemaphoreType.DMA((4,)),
         ],
-        compiler_params=params(40),
-        cost_estimate=cost(2 * count * 2 * FEAT * 8 * HEAD_DIM, 6 * MIB),
+        compiler_params=params(14),
+        cost_estimate=cost(1, 1),
         name="project",
-    )(same, prompt, other, own_gain, other_gain, *near, *far)
+    )(same, prompt, other, *near, *far)
 
 
 def resident_kernel(lengths, queries, keys, values, out, top_out, total_out, sums, tops, totals):
@@ -185,7 +182,7 @@
             jax.ShapeDtypeStruct((8, HEAD_DIM), F32),
         ],
         scratch_shapes=[pltpu.VMEM((HEAD_DIM, HEAD_DIM), F32)] * 3,
-        compiler_params=params(16),
+        compiler_params=params(8),
         cost_estimate=cost(4 * ROWS * GROUPS * CONTEXT * HEAD_DIM, 16 * MIB),
         name="resident",
     )(lengths, queries, keys, values)
@@ -245,8 +242,8 @@
         in_specs=[VMEM] * 7,
         out_specs=[VMEM] * 2,
         out_shape=[jax.ShapeDtypeStruct((count, HEAD_DIM), F32)] * 2,
-        compiler_params=params(24),
-        cost_estimate=cost(20 * count * 256, 2 * MIB),
+        compiler_params=params(10),
+        cost_estimate=cost(1, 1),
         name="finish",
     )(*parts, cosine, sine, bias)
 
@@ -286,15 +283,15 @@
     for flip, queries, out in ((1, far_queries, sent), (0, near_queries, kept)):
 
         def block(step, carry, flip=flip, queries=queries, out=out):
-            for inner in range(4):
-                place = step * 4 + inner
+            for inner in range(8):
+                place = step * 8 + inner
                 replica = place * 2 + (core + flip) % 2
                 summed, stats = attend(replica, queries[place])
                 out[place, 0:HEAD_DIM, :] = summed
                 out[place, HEAD_DIM : HEAD_DIM + STAT, :] = stats
             return carry
 
-        lax.fori_loop(0, 4, block, 0)
+        lax.fori_loop(0, 2, block, 0)
 
 
 def attend(starts, pages, page_rows, place_of, parts, cosine, sine, bias, near, far, done):
@@ -305,8 +302,8 @@
         out_specs=[VMEM, VMEM],
         out_shape=[partial, partial],
         scratch_shapes=[pltpu.VMEM((TOK, HEAD_DIM), F32)] * 2,
-        compiler_params=params(32),
-        cost_estimate=cost(4 * 2048 * 128 * 128, 16 * MIB),
+        compiler_params=params(12),
+        cost_estimate=cost(1, 1),
         name="attend",
     )(pages, page_rows, place_of, *parts, cosine, sine, bias, near, far, *done)
 
@@ -336,8 +333,8 @@
         in_specs=[VMEM, VMEM],
         out_specs=VMEM,
         out_shape=jax.ShapeDtypeStruct((16, HEAD_DIM + STAT, HEAD_DIM), BF16),
-        compiler_params=params(16),
-        cost_estimate=cost(16 * 128 * 128 * 4, 2 * MIB),
+        compiler_params=params(8),
+        cost_estimate=cost(1, 1),
         name="merge",
     )(left, right)
 
@@ -367,8 +364,8 @@
         out_specs=VMEM,
         out_shape=jax.ShapeDtypeStruct((ROWS, GROUPS * HEAD_DIM), BF16),
         scratch_shapes=[pltpu.VMEM((HEAD_DIM, HEAD_DIM), F32)],
-        compiler_params=params(16),
-        cost_estimate=cost(16 * 128 * 128 * 4, MIB),
+        compiler_params=params(8),
+        cost_estimate=cost(1, 1),
         name="conclude",
     )(received, sums, tops, totals)
 
@@ -423,13 +420,17 @@
         return permute(rows, lambda x, y, z, h, c: (x, 1 - y, z, h, c))
 
     def weight_rows(block, follows=None):
-        return lax.dynamic_slice(
+        rows = lax.dynamic_slice(
             after(kv_weight, follows), (0, block * FEAT, 0), (2, FEAT, HEAD_DIM)
         )
+        gain = lax.dynamic_slice(norm_gain, (block * FEAT,), (FEAT,))
+        return (rows.astype(F32) * gain[None, :, None]).astype(BF16)
 
     def fetch(dx, rows):
-        near = permute(rows, lambda x, y, z, h, c: ((x + dx) % 4, y, z, h, c))
-        return near, permute(near, lambda x, y, z, h, c: (x, y, z, h, 1 - c))
+        return permute(rows, lambda x, y, z, h, c: ((x + dx) % 4, y, z, h, c))
+
+    def other_core(rows):
+        return permute(rows, lambda x, y, z, h, c: (x, y, z, h, 1 - c))
 
     def wanted(dx, follows):
         return weight_rows(((x + dx) % 4) * 2 + core, follows)
@@ -440,27 +441,22 @@
     three = wanted(3, first_rows)
     two = wanted(2, (one, three))
     near, far = [None] * 4, [None] * 4
-    near[1], far[1] = fetch(1, one)
-    near[3], far[3] = fetch(3, three)
-    near[2], far[2] = fetch(2, two)
-    query_heads = after(queries, two).reshape(ROWS * GROUPS, HEAD_DIM)
+    near[1], near[3], near[2] = fetch(1, one), fetch(3, three), fetch(2, two)
+    far[2] = other_core(near[2])
+    second_rows = rows_of(1, two)
+    others.append(swap(second_rows))
+    near[0] = weight_rows(x * 2 + core, second_rows)
+    far[0] = weight_rows(x * 2 + 1 - core, second_rows)
+    cosine, sine = angle_tables(after(page_offset, second_rows))
+    query_heads = after(queries, (near[0], far[0], cosine, sine))
+    query_heads = query_heads.reshape(ROWS * GROUPS, HEAD_DIM)
     groups = [[zy * 2 + c for zy in range(16)] for c in range(2)]
     near_queries = lax.all_to_all(
         jnp.broadcast_to(query_heads, (16, ROWS * GROUPS, HEAD_DIM)),
         "rep", 0, 0, tiled=True, axis_index_groups=groups,
     )
-    cosine, sine = angle_tables(page_offset)
-    others.append(swap(rows_of(1, (near[1], cosine, sine))))
-    near[0] = weight_rows(x * 2 + core, (far[1], far[3]))
-    far[0] = weight_rows(x * 2 + 1 - core, (far[1], far[3]))
-    far_queries = permute(
-        after(near_queries, near[2]), lambda x, y, z, h, c: (x, y, z, h, 1 - c)
-    )
-
-    def gain(block):
-        return lax.dynamic_slice(norm_gain, (block * FEAT,), (FEAT,)).reshape(1, FEAT)
-
-    own_gain, other_gain = gain(tp), gain(x * 2 + 1 - y)
+    far[1], far[3] = other_core(near[1]), other_core(near[3])
+
     same = (y == core).astype(jnp.int32).reshape(1)
     bias = kv_bias.astype(F32)
 
@@ -469,19 +465,22 @@
 
     done = []
     for start, other in zip(starts, others):
-        outs = project(same, prompt, start, other, own_gain, other_gain, near, far)
+        outs = project(same, prompt, start, other, near, far)
+        if done:
+            outs, done = lax.optimization_barrier((outs, done))
         parts = [outs[0]] + [
             permute(outs[dx], lambda x, y, z, h, c, dx=dx: ((x - dx) % 4, y, z, h, c))
             for dx in (1, 2, 3)
         ]
         if start != starts[-1]:
             done.extend(finish(parts, cosine, sine, bias, start))
+    far_queries = other_core(after(near_queries, outs[0]))
 
     place_of = core.reshape(1)
     kept, sent = attend(
         starts, pages, page_rows, place_of, parts, cosine, sine, bias, near_queries, far_queries, done
     )
-    arrived = permute(sent, lambda x, y, z, h, c: (x, y, z, h, 1 - c))
+    arrived = other_core(sent)
     merged = merge(kept, arrived)
     received = lax.all_to_all(merged, "rep", 0, 0, tiled=True, axis_index_groups=groups)
     return conclude(received, sums, tops, totals)

time: 124 us -> 124 us (level)
  other arithmetic: 2.65 us -> 9.86 us
  waiting for transfers between devices: 35.3 us -> 40.2 us
  Pallas kernels: 31.5 us -> 27 us
  local copies, waits for them, and re-layouts: 14.1 us -> 10.5 us
  starting transfers between devices: 38.9 us -> 35.7 us
    convert_element_type x0 -> x3, other arithmetic: none -> 7.21 us  [weight_rows(): return (rows.astype(F32) * gain[None, :, None]).astype(BF16)]
    ppermute x16, waiting for transfers between devices: 22.6 us -> 29.1 us  [permute(): return lax.ppermute(array, ('rep', 'tp'), pairs)]
    dynamic_slice x4 -> x1, local copies, waits for them, and re-layouts: 5.12 us -> 0.75 us  [weight_rows(): gain = lax.dynamic_slice(norm_gain, (block * FEAT,), (FEAT,))]
    pallas_call x2, Pallas kernels: 13.2 us -> 10.2 us  [project(): pl.pallas_call(functools.partial(project_kernel, start), in_specs=[SMEM]...]
    ppermute x16, starting transfers between devices: 17.8 us -> 15 us  [permute(): return lax.ppermute(array, ('rep', 'tp'), pairs)]
    all_to_all x1, waiting for transfers between devices: 12.7 us -> 11.1 us  [per_device(): lax.all_to_all(merged, 'rep', 0, 0, tiled=True, axis_index_groups=groups)]
    unnamed x28 -> x30, local copies, waits for them, and re-layouts: 4.46 us -> 5.3 us
  transfers between devices with their start and end apart: 18 -> 18, of which waited for: 9 -> 11; matrix products, arithmetic and copies ran while one was open for 8% -> 10% of each run, Pallas kernels for 17% -> 14%
where the time goes in v3:
time: 124 us
  waiting for transfers between devices  40.2 us (32%)
  starting transfers between devices  35.7 us (29%)
  Pallas kernels  27 us (22%)
  local copies, waits for them, and re-layouts  10.5 us (8%)
  other arithmetic  9.86 us (8%)
    ppermute x16, waiting for transfers between devices, permute(): return lax.ppermute(array, ('rep', 'tp'), pairs)  29.1 us
    ppermute x16, starting transfers between devices, permute(): return lax.ppermute(array, ('rep', 'tp'), pairs)  15 us
    all_to_all x1, waiting for transfers between devices, per_device(): lax.all_to_all(merged, 'rep', 0, 0, tiled=True, axis_index_groups=groups)  11.1 us
    all_to_all x1, starting transfers between devices, per_device(): lax.all_to_all(jnp.broadcast_to(query_heads, (16, ROWS * GROUPS, HEAD_DIM...  10.5 us
    all_to_all x1, starting transfers between devices, per_device(): lax.all_to_all(merged, 'rep', 0, 0, tiled=True, axis_index_groups=groups)  10.3 us
    pallas_call x2, Pallas kernels, project(): pl.pallas_call(functools.partial(project_kernel, start), in_specs=[SMEM]...  10.2 us
    pallas_call x1, Pallas kernels, attend(): pl.pallas_call(functools.partial(attend_kernel, starts), in_specs=[SMEM]...  7.89 us
    convert_element_type x3, other arithmetic, weight_rows(): return (rows.astype(F32) * gain[None, :, None]).astype(BF16)  7.21 us
  transfers between devices with their start and end apart: 18, of which 11 were waited for; matrix products, arithmetic and copies ran while one was open for 10% of the time, Pallas kernels for 14%

profile of v3, /device:TPU:8, one launch (start us, length us, event | category | flops | bytes accessed | tf_op | source)
XLA Modules:
  0.0 123.6 jit_solution(13580678818961155079)
XLA Ops:
  0.0 2.4 %slice.6 = bf16[512,1024]{1,0:T(8,128)(2,1)} slice(bf16[1024,1024]{1,0:T(8,128)(2,1)} %own.3), slice={[0:512], [0:1024]} | slice | bytes 2097152 | tf_op jit(solution)/shard_map/slice | solution.py:417
  2.4 2.2 %collective-permute-start.7 = (bf16[512,1024]{1,0:T(8,128)(2,1)}, bf16[512,1024]{1,0:T(8,128)(2,1)}, u32[]{:S(2)}, u32[]{:S(2)}) collective-permute-start(bf16[512,1024]{1,0:T(8,128)(2,1)} %slice.6), channel_id=1, source_target_pairs={{0,1},{8,9},{16,17},{24,25},{32,33},{40,41},{48,49},{56,57},{64,65... | collective-permute-start | bytes 3145736 | tf_op jit(solution)/shard_map/ppermute | solution.py:56
  4.6 0.8 fusion.2
  5.4 2.5 %multiply_convert_fusion.3 = (bf16[2,1024,128]{2,1,0:T(8,128)(2,1)}, bf16[2,1024,128]{2,1,0:T(8,128)(2,1)}) fusion(f32[1024]{0:T(1024)S(1)} %get-tuple-element.69, bf16[2,8192,128]{2,1,0:T(8,128)(2,1)} %param.13, s32[]{:T(128)S(6)} %select_n.62, f32[1024]{0:T(1024)S(1)} %get-tuple-element.70, s32[]{:T(128)S(6)} %select_n.60), kind=kLoop, calls=%fused_computation.3 | loop fusion | flops 1572864 | bytes 2105352 | tf_op jit(solution)/shard_map/convert_element_type | solution.py:427
  7.9 1.0 collective-permute-start.3
  8.9 1.0 collective-permute-start.1
  9.9 2.1 %multiply_convert_fusion.2 = bf16[2,1024,128]{2,1,0:T(8,128)(2,1)} fusion(f32[1024]{0:T(1024)S(1)} %get-tuple-element.68, bf16[2,8192,128]{2,1,0:T(8,128)(2,1)} %param.13, s32[]{:T(128)S(6)} %select_n.64), kind=kLoop, calls=%fused_computation.2 | loop fusion | flops 786432 | bytes 1052676 | tf_op jit(solution)/shard_map/convert_element_type | solution.py:427
  12.0 1.3 %collective-permute-start.2 = (bf16[2,1024,128]{2,1,0:T(8,128)(2,1)}, bf16[2,1024,128]{2,1,0:T(8,128)(2,1)}, u32[]{:S(2)}, u32[]{:S(2)}) collective-permute-start(bf16[2,1024,128]{2,1,0:T(8,128)(2,1)} %multiply_convert_fusion.2), channel_id=1, source_target_pairs={{0,4},{8,12},{16,20},{24,28},{32,36},{40,44},{48,52},{56,60},{64,6... | collective-permute-start | bytes 1572872 | tf_op jit(solution)/shard_map/ppermute | solution.py:56
  13.3 1.1 slice.7
  14.4 1.6 %collective-permute-start = (bf16[512,1024]{1,0:T(8,128)(2,1)}, bf16[512,1024]{1,0:T(8,128)(2,1)}, u32[]{:S(2)}, u32[]{:S(2)}) collective-permute-start(bf16[512,1024]{1,0:T(8,128)(2,1)} %slice.7), channel_id=1, source_target_pairs={{0,1},{8,9},{16,17},{24,25},{32,33},{40,41},{48,49},{56,57},{64,65... | collective-permute-start | bytes 3145736 | tf_op jit(solution)/shard_map/ppermute | solution.py:56
  16.1 1.9 %fusion = (f32[1024,64]{1,0:T(8,128)S(1)}, f32[1024,64]{1,0:T(8,128)S(1)}, f32[1024,64]{1,0:T(8,128)S(1)}) fusion(f32[64]{0:T(128)S(1)} %multiply_exponential_fusion, f32[1024]{0:T(1024)S(1)} %convert_element_type.59), kind=kLoop, calls=%fused_computation.9 | loop fusion | flops 131072 | bytes 790784 | tf_op jit(solution)/shard_map/neg | solution.py:382
  18.0 2.6 %multiply_convert_fusion = (bf16[2,1024,128]{2,1,0:T(8,128)(2,1)}, bf16[2,1024,128]{2,1,0:T(8,128)(2,1)}) fusion(f32[1024]{0:T(1024)S(1)} %get-tuple-element.67, bf16[2,8192,128]{2,1,0:T(8,128)(2,1)} %param.13, s32[]{:T(128)S(6)} %select_n.66, f32[1024]{0:T(1024)S(1)} %get-tuple-element.71, s32[]{:T(128)S(6)} %select_n.65), kind=kLoop, calls=%fused_computation | loop fusion | flops 1572864 | bytes 2105352 | tf_op jit(solution)/shard_map/convert_element_type | solution.py:427
  20.6 0.3 pad_maximum_fusion
  21.0 0.9 broadcast_in_dim.44
  21.9 10.5 %all-to-all-start = ((bf16[16,128,128]{2,1,0:T(8,128)(2,1)}), bf16[16,128,128]{2,1,0:T(8,128)(2,1)}, u32[]{:S(2)}, u32[]{:S(2)}) async-start(bf16[16,128,128]{2,1,0:T(8,128)(2,1)} %broadcast_in_dim.44), calls=%async_computation | async-start | bytes 1048576 | tf_op jit(solution)/shard_map/all_to_all | solution.py:454
  32.4 1.5 %collective-permute-done.2.refs_2_ = bf16[2,1024,128]{2,1,0:T(8,128)(2,1)} collective-permute-done((bf16[2,1024,128]{2,1,0:T(8,128)(2,1)}, bf16[2,1024,128]{2,1,0:T(8,128)(2,1)}, u32[]{:S(2)}, u32[]{:S(2)}) %collective-permute-start.2) | collective-permute-done | bytes 524320 | tf_op jit(solution)/shard_map/ppermute | solution.py:56
  33.9 0.5 collective-permute-start.6
  34.5 0.3 collective-permute-done.1.refs_1_
  34.8 1.4 %collective-permute-done.5.refs_6_ = bf16[2,1024,128]{2,1,0:T(8,128)(2,1)} collective-permute-done((bf16[2,1024,128]{2,1,0:T(8,128)(2,1)}, bf16[2,1024,128]{2,1,0:T(8,128)(2,1)}, u32[]{:S(2)}, u32[]{:S(2)}) %collective-permute-start.5) | collective-permute-done | bytes 524320 | tf_op jit(solution)/shard_map/ppermute | solution.py:56
  36.2 0.7 collective-permute-done.6.refs_7_
  36.9 0.7 collective-permute-done.4.refs_5_
  37.7 1.0 copy-done.1
  38.7 1.0 copy-done.3
  39.8 5.1 %project.3 = (bf16[528,256]{1,0:T(8,128)(2,1)S(1)}, bf16[528,256]{1,0:T(8,128)(2,1)S(1)}, bf16[528,256]{1,0:T(8,128)(2,1)S(1)}, bf16[528,256]{1,0:T(8,128)(2,1)S(1)}) custom-call(s32[1]{0:T(128)} %bitcast.2.same, bf16[1024,1024]{1,0:T(8,128)(2,1)S(1)} %copy-done, bf16[512,1024]{1,0:T(8,128)(2,1)} %collective-permute-done.7.other, ...), custom_call_target="tpu_custom_call" | custom-call | flops 1 | bytes 1 | tf_op jit(solution)/shard_map/project/pallas_call | solution.py:130
  44.9 0.4 collective-permute-start.8
  45.4 2.1 %collective-permute-start.9 = (bf16[528,256]{1,0:T(8,128)(2,1)S(1)}, bf16[528,256]{1,0:T(8,128)(2,1)S(1)}, u32[]{:S(2)}, u32[]{:S(2)}) collective-permute-start(bf16[528,256]{1,0:T(8,128)(2,1)S(1)} %get-tuple-element.43), channel_id=1, source_target_pairs={{0,4},{8,12},{16,20},{24,28},{32,36},{40,44},{48,52},{56,60},{64,6... | collective-permute-start | bytes 811016 | tf_op jit(solution)/shard_map/ppermute | solution.py:56
  47.4 0.4 collective-permute-start.10
  47.9 7.5 %collective-permute-done.other = bf16[512,1024]{1,0:T(8,128)(2,1)} collective-permute-done((bf16[512,1024]{1,0:T(8,128)(2,1)}, bf16[512,1024]{1,0:T(8,128)(2,1)}, u32[]{:S(2)}, u32[]{:S(2)}) %collective-permute-start) | collective-permute-done | bytes 1048608 | tf_op jit(solution)/shard_map/ppermute | solution.py:56
  55.4 5.1 %project.2 = (bf16[528,256]{1,0:T(8,128)(2,1)S(1)}, bf16[528,256]{1,0:T(8,128)(2,1)S(1)}, bf16[528,256]{1,0:T(8,128)(2,1)S(1)}, bf16[528,256]{1,0:T(8,128)(2,1)S(1)}) custom-call(s32[1]{0:T(128)} %bitcast.2.same, bf16[1024,1024]{1,0:T(8,128)(2,1)S(1)} %copy-done, bf16[512,1024]{1,0:T(8,128)(2,1)} %collective-permute-done.other, ...), custom_call_target="tpu_custom_call" | custom-call | flops 1 | bytes 1 | tf_op jit(solution)/shard_map/project/pallas_call | solution.py:130
  60.5 0.6 collective-permute-done.10.refs_3_
  61.1 0.4 finish.1
  61.5 0.1 collective-permute-start.14
  61.7 0.2 convert_reduce_fusion
  61.8 2.6 %collective-permute-start.11 = (bf16[528,256]{1,0:T(8,128)(2,1)}, bf16[528,256]{1,0:T(8,128)(2,1)S(1)}, u32[]{:S(2)}, u32[]{:S(2)}) collective-permute-start(bf16[528,256]{1,0:T(8,128)(2,1)} %copy-done.9), channel_id=1, source_target_pairs={{0,6},{8,14},{16,22},{24,30},{32,38},{40,46},{48,54},{56,62},{64,7... | collective-permute-start | bytes 811016 | tf_op jit(solution)/shard_map/ppermute | solution.py:56
  64.4 0.8 collective-permute-start.12
  65.2 0.9 collective-permute-start.13
  66.1 0.1 select_reduce_fusion
  66.2 10.7 %collective-permute-done.11.refs_1_ = bf16[528,256]{1,0:T(8,128)(2,1)S(1)} collective-permute-done((bf16[528,256]{1,0:T(8,128)(2,1)}, bf16[528,256]{1,0:T(8,128)(2,1)S(1)}, u32[]{:S(2)}, u32[]{:S(2)}) %collective-permute-start.11) | collective-permute-done | bytes 270368 | tf_op jit(solution)/shard_map/ppermute | solution.py:56
  77.0 3.6 %collective-permute-done.13.refs_3_ = bf16[528,256]{1,0:T(8,128)(2,1)S(1)} collective-permute-done((bf16[528,256]{1,0:T(8,128)(2,1)}, bf16[528,256]{1,0:T(8,128)(2,1)S(1)}, u32[]{:S(2)}, u32[]{:S(2)}) %collective-permute-start.13) | collective-permute-done | bytes 270368 | tf_op jit(solution)/shard_map/ppermute | solution.py:56
  80.5 7.9 %attend.1 = (bf16[16,144,128]{2,1,0:T(8,128)(2,1)S(1)}, bf16[16,144,128]{2,1,0:T(8,128)(2,1)S(1)}) custom-call(s32[256]{0:T(256)S(1)} %get-tuple-element.62.pages, s32[256]{0:T(256)S(1)} %get-tuple-element.61.page_rows, s32[1]{0:T(128)} %bitcast.1.place_of, bf16[528,256]{1,0:T(8,128)(2,1)S(1)} %get-tuple-element.48.refs_0_, ...), custom_call_target="tpu_custom_call" | custom-call | flops 1 | bytes 1 | tf_op jit(solution)/shard_map/attend/pallas_call | solution.py:299
  88.5 2.0 %collective-permute-done.15.right = bf16[16,144,128]{2,1,0:T(8,128)(2,1)S(1)} collective-permute-done((bf16[16,144,128]{2,1,0:T(8,128)(2,1)S(1)}, bf16[16,144,128]{2,1,0:T(8,128)(2,1)S(1)}, u32[]{:S(2)}, u32[]{:S(2)}) %collective-permute-start.15) | collective-permute-done | bytes 589856 | tf_op jit(solution)/shard_map/ppermute | solution.py:56
  90.5 1.2 merge.1
  91.7 10.3 %all-to-all-start.1 = ((bf16[16,144,128]{2,1,0:T(8,128)(2,1)}), bf16[16,144,128]{2,1,0:T(8,128)(2,1)S(1)}, u32[]{:S(2)}, u32[]{:S(2)}) async-start(bf16[16,144,128]{2,1,0:T(8,128)(2,1)} %merge.1), calls=%async_computation.1 | async-start | bytes 1179648 | tf_op jit(solution)/shard_map/all_to_all | solution.py:485
  102.0 1.6 %copy-done.4 = bf16[16,512,128]{2,1,0:T(8,128)(2,1)S(1)} copy-done((bf16[16,512,128]{2,1,0:T(8,128)(2,1)S(1)}, bf16[16,512,128]{2,1,0:T(8,128)(2,1)}, u32[]{:S(2)}) %copy-start.4) | copy-done | bytes 2097176
  103.6 1.6 %copy-done.5 = bf16[16,512,128]{2,1,0:T(8,128)(2,1)S(1)} copy-done((bf16[16,512,128]{2,1,0:T(8,128)(2,1)S(1)}, bf16[16,512,128]{2,1,0:T(8,128)(2,1)}, u32[]{:S(2)}) %copy-start.5) | copy-done | bytes 2097176
  105.2 6.5 %resident.1 = (f32[128,128]{1,0:T(8,128)S(1)}, f32[8,128]{1,0:T(8,128)S(1)}, f32[8,128]{1,0:T(8,128)S(1)}) custom-call(s32[16]{0:T(128)S(1)} %copy-done.6, bf16[128,128]{1,0:T(8,128)(2,1)S(1)} %reshape.49.queries, bf16[16,512,128]{2,1,0:T(8,128)(2,1)S(1)} %copy-done.4, bf16[16,512,128]{2,1,0:T(8,128)(2,1)S(1)} %copy-done.5), custom_call_target="tpu_custom_call" | custom-call | flops 33554432 | bytes 16777216 | tf_op jit(solution)/shard_map/resident/pallas_call | solution.py:174
  111.7 11.1 %all-to-all-done.1.received = bf16[16,144,128]{2,1,0:T(8,128)(2,1)S(1)} async-done(((bf16[16,144,128]{2,1,0:T(8,128)(2,1)}), bf16[16,144,128]{2,1,0:T(8,128)(2,1)S(1)}, u32[]{:S(2)}, u32[]{:S(2)}) %all-to-all-start.1) | async-done | bytes 589856 | tf_op jit(solution)/shard_map/all_to_all | solution.py:485
  122.8 0.9 conclude.1
  (42 shorter events, 0.4 us)
Async XLA Ops:
  0.0 13.3 %copy-start = (bf16[1024,1024]{1,0:T(8,128)(2,1)S(1)}, bf16[1024,1024]{1,0:T(8,128)(2,1)}, u32[]{:S(2)}) copy-start(bf16[1024,1024]{1,0:T(8,128)(2,1)} %own.3) | copy-start | bytes 6291460
  0.0 15.9 %copy-start.11 = (s32[128]{0:T(128)S(1)}, s32[128]{0:T(128)}, u32[]{:S(2)}) copy-start(s32[128]{0:T(128)} %param.17) | copy-start | bytes 1540
  2.4 35.3 %collective-permute-start.7 = (bf16[512,1024]{1,0:T(8,128)(2,1)}, bf16[512,1024]{1,0:T(8,128)(2,1)}, u32[]{:S(2)}, u32[]{:S(2)}) collective-permute-start(bf16[512,1024]{1,0:T(8,128)(2,1)} %slice.6), channel_id=1, source_target_pairs={{0,1},{8,9},{16,17},{24,25},{32,33},{40,41},{48,49},{56,57},{64,65... | collective-permute-start | bytes 3145736 | tf_op jit(solution)/shard_map/ppermute | solution.py:56
  7.9 26.1 %collective-permute-start.3 = (bf16[2,1024,128]{2,1,0:T(8,128)(2,1)}, bf16[2,1024,128]{2,1,0:T(8,128)(2,1)}, u32[]{:S(2)}, u32[]{:S(2)}) collective-permute-start(bf16[2,1024,128]{2,1,0:T(8,128)(2,1)} %get-tuple-element.65), channel_id=1, source_target_pairs={{0,6},{8,14},{16,22},{24,30},{32,38},{40,46},{48,54},{56,62},{64,7... | collective-permute-start | bytes 1572872 | tf_op jit(solution)/shard_map/ppermute | solution.py:56
  8.9 25.9 %collective-permute-start.1 = (bf16[2,1024,128]{2,1,0:T(8,128)(2,1)}, bf16[2,1024,128]{2,1,0:T(8,128)(2,1)}, u32[]{:S(2)}, u32[]{:S(2)}) collective-permute-start(bf16[2,1024,128]{2,1,0:T(8,128)(2,1)} %get-tuple-element.66), channel_id=1, source_target_pairs={{0,2},{8,10},{16,18},{24,26},{32,34},{40,42},{48,50},{56,58},{64,6... | collective-permute-start | bytes 1572872 | tf_op jit(solution)/shard_map/ppermute | solution.py:56
  12.0 9.0 %copy-start.10 = (bf16[16,1024]{1,0:T(8,128)(2,1)S(1)}, bf16[16,1024]{1,0:T(8,128)(2,1)}, u32[]{:S(2)}) copy-start(bf16[16,1024]{1,0:T(8,128)(2,1)} %param.18) | copy-start | bytes 98308
  12.0 21.9 %collective-permute-start.2 = (bf16[2,1024,128]{2,1,0:T(8,128)(2,1)}, bf16[2,1024,128]{2,1,0:T(8,128)(2,1)}, u32[]{:S(2)}, u32[]{:S(2)}) collective-permute-start(bf16[2,1024,128]{2,1,0:T(8,128)(2,1)} %multiply_convert_fusion.2), channel_id=1, source_target_pairs={{0,4},{8,12},{16,20},{24,28},{32,36},{40,44},{48,52},{56,60},{64,6... | collective-permute-start | bytes 1572872 | tf_op jit(solution)/shard_map/ppermute | solution.py:56
  14.4 41.0 %collective-permute-start = (bf16[512,1024]{1,0:T(8,128)(2,1)}, bf16[512,1024]{1,0:T(8,128)(2,1)}, u32[]{:S(2)}, u32[]{:S(2)}) collective-permute-start(bf16[512,1024]{1,0:T(8,128)(2,1)} %slice.7), channel_id=1, source_target_pairs={{0,1},{8,9},{16,17},{24,25},{32,33},{40,41},{48,49},{56,57},{64,65... | collective-permute-start | bytes 3145736 | tf_op jit(solution)/shard_map/ppermute | solution.py:56
  21.9 25.9 %copy-start.13 = (bf16[2,128]{1,0:T(2,128)(2,1)S(1)}, bf16[2,128]{1,0:T(2,128)(2,1)}, u32[]{:S(2)}) copy-start(bf16[2,128]{1,0:T(2,128)(2,1)} %param.14) | copy-start | bytes 1540
  21.9 39.6 %all-to-all-start = ((bf16[16,128,128]{2,1,0:T(8,128)(2,1)}), bf16[16,128,128]{2,1,0:T(8,128)(2,1)}, u32[]{:S(2)}, u32[]{:S(2)}) async-start(bf16[16,128,128]{2,1,0:T(8,128)(2,1)} %broadcast_in_dim.44), calls=%async_computation | async-start | bytes 1048576 | tf_op jit(solution)/shard_map/all_to_all | solution.py:454
  33.9 2.3 %collective-permute-start.5 = (bf16[2,1024,128]{2,1,0:T(8,128)(2,1)}, bf16[2,1024,128]{2,1,0:T(8,128)(2,1)}, u32[]{:S(2)}, u32[]{:S(2)}) collective-permute-start(bf16[2,1024,128]{2,1,0:T(8,128)(2,1)} %collective-permute-done.2.refs_2_), channel_id=1, source_target_pairs={{0,8},{8,0},{16,24},{24,16},{32,40},{40,32},{48,56},{56,48},{64,72... | collective-permute-start | bytes 1572872 | tf_op jit(solution)/shard_map/ppermute | solution.py:56
  33.9 3.0 %collective-permute-start.6 = (bf16[2,1024,128]{2,1,0:T(8,128)(2,1)}, bf16[2,1024,128]{2,1,0:T(8,128)(2,1)}, u32[]{:S(2)}, u32[]{:S(2)}) collective-permute-start(bf16[2,1024,128]{2,1,0:T(8,128)(2,1)} %collective-permute-done.3.refs_3_), channel_id=1, source_target_pairs={{0,8},{8,0},{16,24},{24,16},{32,40},{40,32},{48,56},{56,48},{64,72... | collective-permute-start | bytes 1572872 | tf_op jit(solution)/shard_map/ppermute | solution.py:56
  34.8 2.9 %collective-permute-start.4 = (bf16[2,1024,128]{2,1,0:T(8,128)(2,1)}, bf16[2,1024,128]{2,1,0:T(8,128)(2,1)}, u32[]{:S(2)}, u32[]{:S(2)}) collective-permute-start(bf16[2,1024,128]{2,1,0:T(8,128)(2,1)} %collective-permute-done.1.refs_1_), channel_id=1, source_target_pairs={{0,8},{8,0},{16,24},{24,16},{32,40},{40,32},{48,56},{56,48},{64,72... | collective-permute-start | bytes 1572872 | tf_op jit(solution)/shard_map/ppermute | solution.py:56
  37.7 1.0 copy-start.1
  38.7 1.0 copy-start.3
  39.8 15.6 %copy-start.2 = (bf16[2,1024,128]{2,1,0:T(8,128)(2,1)S(1)}, bf16[2,1024,128]{2,1,0:T(8,128)(2,1)}, u32[]{:S(2)}) copy-start(bf16[2,1024,128]{2,1,0:T(8,128)(2,1)} %get-tuple-element.63.refs_4_) | copy-start | bytes 1572868
  44.9 15.6 %collective-permute-start.8 = (bf16[528,256]{1,0:T(8,128)(2,1)S(1)}, bf16[528,256]{1,0:T(8,128)(2,1)S(1)}, u32[]{:S(2)}, u32[]{:S(2)}) collective-permute-start(bf16[528,256]{1,0:T(8,128)(2,1)S(1)} %get-tuple-element.42), channel_id=1, source_target_pairs={{0,6},{8,14},{16,22},{24,30},{32,38},{40,46},{48,54},{56,62},{64,7... | collective-permute-start | bytes 811016 | tf_op jit(solution)/shard_map/ppermute | solution.py:56
  45.4 15.1 %collective-permute-start.9 = (bf16[528,256]{1,0:T(8,128)(2,1)S(1)}, bf16[528,256]{1,0:T(8,128)(2,1)S(1)}, u32[]{:S(2)}, u32[]{:S(2)}) collective-permute-start(bf16[528,256]{1,0:T(8,128)(2,1)S(1)} %get-tuple-element.43), channel_id=1, source_target_pairs={{0,4},{8,12},{16,20},{24,28},{32,36},{40,44},{48,52},{56,60},{64,6... | collective-permute-start | bytes 811016 | tf_op jit(solution)/shard_map/ppermute | solution.py:56
  47.4 13.7 %collective-permute-start.10 = (bf16[528,256]{1,0:T(8,128)(2,1)S(1)}, bf16[528,256]{1,0:T(8,128)(2,1)S(1)}, u32[]{:S(2)}, u32[]{:S(2)}) collective-permute-start(bf16[528,256]{1,0:T(8,128)(2,1)S(1)} %get-tuple-element.44), channel_id=1, source_target_pairs={{0,2},{8,10},{16,18},{24,26},{32,34},{40,42},{48,50},{56,58},{64,6... | collective-permute-start | bytes 811016 | tf_op jit(solution)/shard_map/ppermute | solution.py:56
  47.9 13.8 %copy-start.14 = (s32[128,1]{0,1:T(1,128)S(1)}, s32[128,1]{0,1:T(1,128)}, u32[]{:S(2)}) copy-start(s32[128,1]{0,1:T(1,128)} %param.15) | copy-start | bytes 1540
  47.9 18.2 %copy-start.12 = (s32[128]{0:T(128)S(1)}, s32[128]{0:T(128)}, u32[]{:S(2)}) copy-start(s32[128]{0:T(128)} %param.16) | copy-start | bytes 1540
  60.5 1.0 copy-start.7
  60.5 1.0 copy-start.8
  60.5 1.0 copy-start.9
  61.1 40.9 %copy-start.6 = (s32[16]{0:T(128)S(1)}, s32[16]{0:T(128)}, u32[]{:S(2)}) copy-start(s32[16]{0:T(128)} %lengths.1) | copy-start | bytes 196
  61.5 19.0 %collective-permute-start.14 = (bf16[16,128,128]{2,1,0:T(8,128)(2,1)}, bf16[16,128,128]{2,1,0:T(8,128)(2,1)S(1)}, u32[]{:S(2)}, u32[]{:S(2)}) collective-permute-start(bf16[16,128,128]{2,1,0:T(8,128)(2,1)} %all-to-all-done.refs_7_), channel_id=1, source_target_pairs={{0,8},{8,0},{16,24},{24,16},{32,40},{40,32},{48,56},{56,48},{64,72... | collective-permute-start | bytes 1572872 | tf_op jit(solution)/shard_map/ppermute | solution.py:56
  61.8 15.1 %collective-permute-start.11 = (bf16[528,256]{1,0:T(8,128)(2,1)}, bf16[528,256]{1,0:T(8,128)(2,1)S(1)}, u32[]{:S(2)}, u32[]{:S(2)}) collective-permute-start(bf16[528,256]{1,0:T(8,128)(2,1)} %copy-done.9), channel_id=1, source_target_pairs={{0,6},{8,14},{16,22},{24,30},{32,38},{40,46},{48,54},{56,62},{64,7... | collective-permute-start | bytes 811016 | tf_op jit(solution)/shard_map/ppermute | solution.py:56
  64.4 12.6 %collective-permute-start.12 = (bf16[528,256]{1,0:T(8,128)(2,1)}, bf16[528,256]{1,0:T(8,128)(2,1)S(1)}, u32[]{:S(2)}, u32[]{:S(2)}) collective-permute-start(bf16[528,256]{1,0:T(8,128)(2,1)} %copy-done.8), channel_id=1, source_target_pairs={{0,4},{8,12},{16,20},{24,28},{32,36},{40,44},{48,52},{56,60},{64,6... | collective-permute-start | bytes 811016 | tf_op jit(solution)/shard_map/ppermute | solution.py:56
  65.2 15.3 %collective-permute-start.13 = (bf16[528,256]{1,0:T(8,128)(2,1)}, bf16[528,256]{1,0:T(8,128)(2,1)S(1)}, u32[]{:S(2)}, u32[]{:S(2)}) collective-permute-start(bf16[528,256]{1,0:T(8,128)(2,1)} %copy-done.7), channel_id=1, source_target_pairs={{0,2},{8,10},{16,18},{24,26},{32,34},{40,42},{48,50},{56,58},{64,6... | collective-permute-start | bytes 811016 | tf_op jit(solution)/shard_map/ppermute | solution.py:56
  88.4 2.1 %collective-permute-start.15 = (bf16[16,144,128]{2,1,0:T(8,128)(2,1)S(1)}, bf16[16,144,128]{2,1,0:T(8,128)(2,1)S(1)}, u32[]{:S(2)}, u32[]{:S(2)}) collective-permute-start(bf16[16,144,128]{2,1,0:T(8,128)(2,1)S(1)} %get-tuple-element.57), channel_id=1, source_target_pairs={{0,8},{8,0},{16,24},{24,16},{32,40},{40,32},{48,56},{56,48},{64,72... | collective-permute-start | bytes 1769480 | tf_op jit(solution)/shard_map/ppermute | solution.py:56
  91.7 31.1 %all-to-all-start.1 = ((bf16[16,144,128]{2,1,0:T(8,128)(2,1)}), bf16[16,144,128]{2,1,0:T(8,128)(2,1)S(1)}, u32[]{:S(2)}, u32[]{:S(2)}) async-start(bf16[16,144,128]{2,1,0:T(8,128)(2,1)} %merge.1), calls=%async_computation.1 | async-start | bytes 1179648 | tf_op jit(solution)/shard_map/all_to_all | solution.py:485
  102.0 1.6 %copy-start.4 = (bf16[16,512,128]{2,1,0:T(8,128)(2,1)S(1)}, bf16[16,512,128]{2,1,0:T(8,128)(2,1)}, u32[]{:S(2)}) copy-start(bf16[16,512,128]{2,1,0:T(8,128)(2,1)} %keys.1) | copy-start | bytes 6291460
  103.6 1.6 %copy-start.5 = (bf16[16,512,128]{2,1,0:T(8,128)(2,1)S(1)}, bf16[16,512,128]{2,1,0:T(8,128)(2,1)}, u32[]{:S(2)}) copy-start(bf16[16,512,128]{2,1,0:T(8,128)(2,1)} %values.1) | copy-start | bytes 6291460
